TPU v7x, 512 devices: a whole 4x4x16 slice. The times are simulated.
512 devices in a mesh: hist: 128 (over z, x, core), mp: 4 (over y).
Axes of the slice: x: 4, y: 4, z: 16, core: 2. Of those that a mesh axis runs over, the one named last changes fastest.
Arguments:
- candidates: bfloat16 [1024, 1024], P('hist'), may hold values from -6 to 6
- actions: bfloat16 [256, 1024], P('hist'), may hold values from -6 to 6
- hist_keys: bfloat16 [131072, 1024], P('hist', 'mp'), may hold values from -6 to 6
- hist_values: bfloat16 [131072, 1024], P('hist', 'mp'), may hold values from -6 to 6
- w_query: bfloat16 [1024, 1024], P(None, 'mp'), may hold values from -0.1875 to 0.1875
- w_gate: bfloat16 [1024, 1024], P(None, 'mp'), may hold values from -0.1875 to 0.1875
- w_key: bfloat16 [1024, 1024], P(None, 'mp'), may hold values from -0.1875 to 0.1875
- w_value: bfloat16 [1024, 1024], P(None, 'mp'), may hold values from -0.1875 to 0.1875
- w_out: bfloat16 [1024, 1024], P('mp'), may hold values from -0.1875 to 0.1875
- segment_list: int32 [4, 128], replicated, may hold values from -1 to 255, as said below
- segment_count: int32 [4], replicated, may hold values from 1 to 128, as said below
- segment_length: int32 [256], replicated, may hold values from 128 to 448
- new_count: int32 [4], replicated, may hold values from 1 to 64
- batch_user: int32 [128], replicated, may hold values from 0 to 3
Outputs:
- ranked: bfloat16 [1024, 1024], P('hist', 'mp')
- new_keys: bfloat16 [131072, 1024], P('hist', 'mp')
- new_values: bfloat16 [131072, 1024], P('hist', 'mp')
Inputs may be any that keep to these rules, and one draw needn't show every extreme that they name: `segment_list`: row u lists (segment_count)[u] distinct segment ids and then -1; every id of 0 to 255 is listed by exactly one user; the last listed segment of a user receives its new actions. `segment_count`: the counts sum to 256; one user lists exactly 128 segments.
All inputs are finite; a program needn't handle non-finite values.
Results may differ from a plain program's by a relative error of at most 0.0045.
Values may be sent and summed in bfloat16 or wider, within the bound.
No kernel may reach another device: no remote copies, remote signals or barrier semaphores. Data moves between devices by JAX's collectives and lax.ppermute only.
A program may use at most 64 MiB of HBM per device.

v0:
```python
import math

import jax
import jax.numpy as jnp
from jax import lax
from jax.sharding import PartitionSpec as P

D = 1024
DH = 128
SEG = 512
NEW = 64
USERS = 4


def per_device(
    candidates,
    actions,
    hist_keys,
    hist_values,
    w_query,
    w_gate,
    w_key,
    w_value,
    w_out,
    segment_list,
    segment_count,
    segment_length,
    new_count,
    batch_user,
):
    device = lax.axis_index("hist")
    device_count = lax.axis_size("hist")
    model_part = lax.axis_index("mp")
    batch_rows = candidates.shape[0]
    local_width = w_query.shape[1]
    local_heads = local_width // DH
    local_segs = hist_keys.shape[0] // SEG
    action_count = actions.shape[0]
    arriving = device_count * action_count
    logit_scale = 1.0 / math.sqrt(DH)
    user_ids = jnp.arange(USERS, dtype=jnp.int32)
    last_segment = jnp.take_along_axis(segment_list, (segment_count - 1)[:, None], axis=1)[:, 0]
    fresh_keys = jnp.dot(actions, w_key, preferred_element_type=jnp.float32).astype(jnp.bfloat16)
    fresh_values = jnp.dot(actions, w_value, preferred_element_type=jnp.float32).astype(
        jnp.bfloat16
    )
    fresh_rows = jnp.concatenate([fresh_keys, fresh_values], axis=1)
    own_rows = device * action_count + jnp.arange(action_count, dtype=jnp.int32)
    own_user = own_rows // NEW
    target_seg = jnp.sum(
        jnp.where(own_user[:, None] == user_ids[None, :], last_segment[None, :], 0), axis=1
    )
    target_dev = target_seg // local_segs
    chosen_dev = target_dev[None, :] == jnp.arange(device_count, dtype=jnp.int32)[:, None]
    outgoing = jnp.where(
        chosen_dev[:, :, None], fresh_rows[None, :, :], jnp.zeros((), jnp.bfloat16)
    )
    incoming = lax.all_to_all(outgoing, "hist", split_axis=0, concat_axis=0, tiled=True).reshape(
        arriving, 2 * local_width
    )
    arrival_ids = jnp.arange(arriving, dtype=jnp.int32)
    arrival_user = arrival_ids // NEW
    arrival_step = arrival_ids % NEW
    arrival_hot = arrival_user[:, None] == user_ids[None, :]
    arrival_limit = jnp.sum(jnp.where(arrival_hot, new_count[None, :], 0), axis=1)
    global_ids = device * local_segs + jnp.arange(local_segs, dtype=jnp.int32)
    open_hot = last_segment[None, :] == global_ids[:, None]
    local_length = lax.dynamic_slice_in_dim(segment_length, device * local_segs, local_segs)
    receives = jnp.any(open_hot[:, None, :] & arrival_hot[None, :, :], axis=2)
    receives = receives & (arrival_step < arrival_limit)[None, :]
    target_row = local_length[:, None] + arrival_step[None, :]
    positions = jnp.arange(SEG, dtype=jnp.int32)
    placing = (positions[None, :, None] == target_row[:, None, :]) & receives[:, None, :]
    placed = jnp.einsum(
        "lpi,ic->lpc", placing.astype(jnp.bfloat16), incoming, preferred_element_type=jnp.float32
    ).astype(jnp.bfloat16)
    stored = jnp.concatenate([hist_keys, hist_values], axis=1).reshape(
        local_segs, SEG, 2 * local_width
    )
    updated = jnp.where(jnp.any(placing, axis=2)[:, :, None], placed, stored)
    added_rows = jnp.sum(jnp.where(open_hot, new_count[None, :], 0), axis=1)
    key_mask = (positions[None, :] < (local_length + added_rows)[:, None]).astype(jnp.float32)
    owner_hot = jnp.any(segment_list[None, :, :] == global_ids[:, None, None], axis=2).astype(
        jnp.float32
    )
    batch_hot = (batch_user[:, None] == user_ids[None, :]).astype(jnp.float32)
    pair_mask = jnp.dot(batch_hot, owner_hot.T)
    seg_keys = updated[:, :, :local_width].reshape(local_segs, SEG, local_heads, DH)
    segment_value_rows = updated[:, :, local_width:].reshape(local_segs, SEG, local_heads, DH)
    queries = jnp.dot(candidates, w_query, preferred_element_type=jnp.float32).astype(jnp.bfloat16)
    gate_values = jax.nn.silu(jnp.dot(candidates, w_gate, preferred_element_type=jnp.float32))

    def score_block(packed):
        row_block, first_row = packed
        block_size = row_block.shape[0]
        source = (first_row + jnp.arange(block_size, dtype=jnp.int32)) // batch_rows
        chosen = (source[:, None] == jnp.arange(device_count, dtype=jnp.int32)[None, :]).astype(
            jnp.float32
        )
        row_mask = jnp.dot(chosen, pair_mask)
        query_heads = row_block.reshape(block_size, local_heads, DH)
        partial_list = []
        for segment_position in range(local_segs):
            attention_logits = (
                jnp.einsum(
                    "zoq,eoq->oze",
                    query_heads,
                    seg_keys[segment_position],
                    preferred_element_type=jnp.float32,
                )
                * logit_scale
            )
            attention_weight = (
                jax.nn.silu(attention_logits)
                * key_mask[segment_position][None, None, :]
                * row_mask[:, segment_position][None, :, None]
            ).astype(jnp.bfloat16)
            seg_part = jnp.einsum(
                "lne,eli->nli",
                attention_weight,
                segment_value_rows[segment_position],
                preferred_element_type=jnp.float32,
            )
            partial_list.append(seg_part.reshape(block_size, local_width))
        block_out = jnp.stack(partial_list, axis=1).reshape(
            block_size // batch_rows, batch_rows, local_segs, local_width
        )
        return block_out

    query_piece = lax.all_gather(queries, "hist", axis=0, tiled=True)
    total_rows = query_piece.shape[0]
    block_size = math.gcd(total_rows, 512)
    block_count = total_rows // block_size
    first_rows = jnp.arange(block_count, dtype=jnp.int32) * block_size
    result = lax.map(
        score_block, (query_piece.reshape(block_count, block_size, local_width), first_rows)
    )
    partial_sums = result.reshape((total_rows // batch_rows,) + result.shape[2:])
    returned = lax.all_to_all(partial_sums, "hist", split_axis=0, concat_axis=0, tiled=True)
    attention = jnp.sum(returned, axis=(0, 2))
    row_sum = jnp.sum(attention, axis=1)
    row_squares = jnp.sum(attention * attention, axis=1)
    row_sum, row_squares = lax.psum((row_sum, row_squares), "mp")
    row_mean = row_sum / D
    variance = row_squares / D - row_mean * row_mean
    normed = (attention - row_mean[:, None]) * lax.rsqrt(variance[:, None] + 1e-05)
    mixed_rows = (normed * gate_values).astype(jnp.bfloat16)
    out_terms = jnp.dot(mixed_rows, w_out, preferred_element_type=jnp.float32)
    projected = lax.psum_scatter(out_terms, "mp", scatter_dimension=1, tiled=True)
    residual = lax.dynamic_slice_in_dim(
        candidates, model_part * local_width, local_width, 1
    ).astype(jnp.float32)
    ranked = (residual + projected).astype(jnp.bfloat16)
    new_keys = updated[:, :, :local_width].reshape(local_segs * SEG, local_width)
    new_values = updated[:, :, local_width:].reshape(local_segs * SEG, local_width)
    return (ranked, new_keys, new_values)


def solution(mesh):
    in_specs = (
        P("hist", None),
        P("hist", None),
        P("hist", "mp"),
        P("hist", "mp"),
        P(None, "mp"),
        P(None, "mp"),
        P(None, "mp"),
        P(None, "mp"),
        P("mp", None),
        P(),
        P(),
        P(),
        P(),
        P(),
    )
    out_specs = (P("hist", "mp"), P("hist", "mp"), P("hist", "mp"))
    return jax.shard_map(
        per_device, mesh=mesh, in_specs=in_specs, out_specs=out_specs, check_vma=False
    )
```

profile of v0, /device:TPU:6, one launch (start us, length us, event | category | flops | bytes accessed | tf_op | source)
XLA Modules:
  0.0 292.0 jit_solution(8504824685772142575)
XLA Ops:
  7.2 0.0 copy-start
  7.2 0.0 copy-start.1
  7.2 0.0 copy-start.9
  7.3 0.8 fusion.49
  8.1 1.3 gather_fusion
  9.4 0.7 and_select_fusion.3
  10.1 0.9 select_reduce_fusion.1
  11.0 1.2 convolution_convert_fusion.2
  12.2 1.2 convolution_convert_fusion.3
  13.5 1.0 broadcast_select_fusion
  14.5 19.4 %all-to-all-start = ((bf16[128,2,512]{2,1,0:T(2,128)(2,1)}), bf16[128,2,512]{2,1,0:T(2,128)(2,1)S(1)}, u32[]{:S(2)}, u32[]{:S(2)}) async-start(bf16[128,2,512]{2,1,0:T(2,128)(2,1)} %broadcast_select_fusion), calls=%async_computation | async-start | bytes 524288 | tf_op jit(solution)/shard_map/all_to_all | solution.py:58
  33.9 0.0 reduce-scatter.2.cloned.1.call-start
  34.0 0.0 copy-done.9
  34.0 0.1 select_reduce_fusion
  34.1 0.2 compare_reduce_fusion
  34.3 0.2 convolution_convert_fusion.1
  34.5 87.9 %all_gather.3 = bf16[1024,256]{1,0:T(8,128)(2,1)S(1)} all-gather(bf16[8,256]{1,0:T(8,128)(2,1)S(1)} %convolution_convert_fusion.1), channel_id=1, replica_groups=mesh['hist'=128,'mp'=4] {'hist'}, dimensions={0}, use_global_device_ids=true | all-gather | bytes 528384 | tf_op jit(solution)/shard_map/all_gather | solution.py:130
  122.4 0.1 and_reduce_fusion
  122.5 0.0 copy-done.10
  122.5 0.1 fusion.51
  122.6 0.1 broadcast_add_fusion
  122.7 0.2 fusion.36
  122.9 0.1 pad_maximum_fusion.1
  123.0 0.2 fusion.39
  123.2 0.1 compare_convert_fusion
  123.3 0.0 all-to-all-done
  123.3 0.1 reshape.299
  123.4 0.5 fusion.33
  123.9 1.3 fusion.54
  125.1 0.1 copy.55
  125.2 0.1 copy.56
  125.3 13.7 %while.12 = (s32[]{:T(128)}, f32[2,64,8,2,256]{4,2,3,1,0:T(8,128)}, bf16[2,512,256]{2,1,0:T(8,128)(2,1)S(1)}, bf16[2,512,2,128]{3,1,2,0:T(8,128)(2,1)S(1)}, f32[...) while((s32[]{:T(128)}, f32[2,64,8,2,256]{4,2,3,1,0:T(8,128)}, ...), condition=%wide.region_7.8_spmd, body=%wide.region_6.7_spmd.sunk | while | flops 545857536 | bytes 14189737 | solution.py:135
  125.4 0.7 dynamic_slice.28
  126.0 0.6 add_select_fusion.2
  126.7 0.2 fusion.90
  127.0 0.1 copy.62
  127.1 1.1 fusion.94
  128.2 0.4 copy.64
  128.7 0.4 stack.10
  129.1 1.1 fusion.93
  130.2 0.4 copy.63
  130.6 0.4 stack.9
  131.1 1.1 copy_dynamic-update-slice_fusion.2
  132.1 0.1 copy-done.5
  132.2 0.7 dynamic_slice.28
  132.9 0.6 add_select_fusion.2
  133.5 0.2 fusion.90
  133.8 0.1 copy.62
  134.0 1.1 fusion.94
  135.1 0.4 copy.64
  135.5 0.4 stack.10
  136.0 1.1 fusion.93
  137.1 0.4 copy.63
  137.5 0.4 stack.9
  137.9 1.1 copy_dynamic-update-slice_fusion.2
  139.0 0.0 copy-done.5
  139.1 111.4 %all_to_all.10 = f32[128,8,2,256]{3,1,2,0:T(8,128)S(1)} all-to-all(f32[128,8,2,256]{3,1,2,0:T(8,128)} %bitcast.92), channel_id=1, replica_groups=mesh['hist'=128,'mp'=4] {'hist'}, dimensions={0} | all-to-all | bytes 4194304 | tf_op jit(solution)/shard_map/all_to_all | solution.py:139
  250.5 0.7 fusion.50
  251.1 0.1 multiply_reduce_fusion
  251.2 10.7 %all-reduce = (f32[8]{0:T(128)S(1)}, f32[8]{0:T(128)S(1)}) all-reduce(f32[8]{0:T(128)S(1)} %multiply_reduce_fusion, f32[8]{0:T(128)S(1)} %get-tuple-element.138), channel_id=1, replica_groups=mesh['hist'=128,'mp'=4] {'mp'}, use_global_device_ids=true, to_apply=%region_12.13 | all-reduce | flops 16 | bytes 128 | tf_op jit(solution)/shard_map/psum | solution.py:143
  262.0 1.1 fusion.41
  263.1 0.0 reduce-scatter.2.cloned.1.call-update
  263.1 20.8 %reduce-scatter.2.cloned.1.call-done = f32[8,256]{1,0:T(8,128)} async-done(((f32[8,1024]{1,0:T(8,128)}), f32[8,256]{1,0:T(8,128)}) %reduce-scatter.2.cloned.1.call-update) | async-done | bytes 8208 | tf_op jit(solution)/shard_map/reduce_scatter | solution.py:149
  283.9 1.3 add_convert_fusion
  (42 shorter events, 0.2 us)
Async XLA Ops:
  7.2 254.8 %copy-start = (bf16[256,1024]{1,0:T(8,128)(2,1)S(1)}, bf16[256,1024]{1,0:T(8,128)(2,1)}, u32[]{:S(2)}) copy-start(bf16[256,1024]{1,0:T(8,128)(2,1)} %param.24) | copy-start | bytes 1572868
  7.2 26.9 %copy-start.1 = (s32[4,128]{1,0:T(4,128)S(1)}, s32[4,128]{1,0:T(4,128)}, u32[]{:S(2)}) copy-start(s32[4,128]{1,0:T(4,128)} %param.25) | copy-start | bytes 6148
  7.2 26.8 %copy-start.9 = (s32[4]{0:T(128)S(1)}, s32[4]{0:T(128)}, u32[]{:S(2)}) copy-start(s32[4]{0:T(128)} %param.28) | copy-start | bytes 52
  7.2 27.1 %copy-start.8 = (bf16[8,1024]{1,0:T(8,128)(2,1)S(1)}, bf16[8,1024]{1,0:T(8,128)(2,1)}, u32[]{:S(2)}) copy-start(bf16[8,1024]{1,0:T(8,128)(2,1)} %param.16) | copy-start | bytes 49156
  7.2 27.1 %copy-start.3 = (bf16[1024,256]{1,0:T(8,128)(2,1)S(1)}, bf16[1024,256]{1,0:T(8,128)(2,1)}, u32[]{:S(2)}) copy-start(bf16[1024,256]{1,0:T(8,128)(2,1)} %param.20) | copy-start | bytes 1572868
  7.2 115.3 %copy-start.10 = (s32[256]{0:T(256)S(1)}, s32[256]{0:T(256)}, u32[]{:S(2)}) copy-start(s32[256]{0:T(256)} %param.27) | copy-start | bytes 3076
  7.2 115.7 %copy-start.7 = (bf16[1024,256]{1,0:T(8,128)(2,1)S(1)}, bf16[1024,256]{1,0:T(8,128)(2,1)}, u32[]{:S(2)}) copy-start(bf16[1024,256]{1,0:T(8,128)(2,1)} %param.18) | copy-start | bytes 1572868
  7.2 115.7 %copy-start.6 = (bf16[1024,256]{1,0:T(8,128)(2,1)S(1)}, bf16[1024,256]{1,0:T(8,128)(2,1)}, u32[]{:S(2)}) copy-start(bf16[1024,256]{1,0:T(8,128)(2,1)} %param.19) | copy-start | bytes 1572868
  13.5 109.5 %copy-start.11 = (s32[128]{0:T(128)S(1)}, s32[128]{0:T(128)}, u32[]{:S(2)}) copy-start(s32[128]{0:T(128)} %param.29) | copy-start | bytes 1540
  14.5 108.8 %all-to-all-start = ((bf16[128,2,512]{2,1,0:T(2,128)(2,1)}), bf16[128,2,512]{2,1,0:T(2,128)(2,1)S(1)}, u32[]{:S(2)}, u32[]{:S(2)}) async-start(bf16[128,2,512]{2,1,0:T(2,128)(2,1)} %broadcast_select_fusion), calls=%async_computation | async-start | bytes 524288 | tf_op jit(solution)/shard_map/all_to_all | solution.py:58
  33.9 250.0 %reduce-scatter.2.cloned.1.call-start = ((), (), s32[]{:S(2)}) async-start(), calls=%async_computation.3 | async-start | bytes 40960 | tf_op jit(solution)/shard_map/reduce_scatter | solution.py:149
  125.4 3.7 %copy-start.4 = (bf16[2,512,2,128]{3,1,2,0:T(8,128)(2,1)}, bf16[2,512,2,128]{3,1,2,0:T(8,128)(2,1)S(1)}, u32[]{:S(2)}) copy-start(bf16[2,512,2,128]{3,1,2,0:T(8,128)(2,1)S(1)} %get-tuple-element.253) | copy-start | bytes 1572868 | tf_op jit(solution)/shard_map/while
  131.1 1.2 copy-start.5
  132.2 3.7 %copy-start.4 = (bf16[2,512,2,128]{3,1,2,0:T(8,128)(2,1)}, bf16[2,512,2,128]{3,1,2,0:T(8,128)(2,1)S(1)}, u32[]{:S(2)}) copy-start(bf16[2,512,2,128]{3,1,2,0:T(8,128)(2,1)S(1)} %get-tuple-element.253) | copy-start | bytes 1572868 | tf_op jit(solution)/shard_map/while
  137.9 1.2 copy-start.5
  250.5 11.5 %copy-start.2 = (bf16[1024,256]{1,0:T(8,128)(2,1)S(1)}, bf16[1024,256]{1,0:T(8,128)(2,1)}, u32[]{:S(2)}) copy-start(bf16[1024,256]{1,0:T(8,128)(2,1)} %param.21) | copy-start | bytes 1572868
Sparse Core Ops, SparseCore 0:
  263.2 20.6 reduce-scatter.1
where the time goes:
time: 293 us; the launch traced here: 292 us
  blocking collectives  210 us (72%)
  waiting for transfers between devices  20.8 us (7%)
  starting transfers between devices  19.4 us (7%)
  between operations  14.3 us (5%)
  other arithmetic  9.87 us (3%)
  matrix products  9.37 us (3%)
  local copies, waits for them, and re-layouts  8.08 us (3%)
    all_to_all x1, blocking collectives, per_device(): lax.all_to_all(partial_sums, 'hist', split_axis=0, concat_axis=0, tiled=T...  111 us
    all_gather x1, blocking collectives, per_device(): query_piece = lax.all_gather(queries, 'hist', axis=0, tiled=True)  87.9 us
    reduce_scatter x1, waiting for transfers between devices, per_device(): lax.psum_scatter(out_terms, 'mp', scatter_dimension=1, tiled=True)  20.8 us
    all_to_all x1, starting transfers between devices, per_device(): lax.all_to_all(outgoing, 'hist', split_axis=0, concat_axis=0, tiled=True)  19.4 us
    psum x1, blocking collectives, per_device(): row_sum, row_squares = lax.psum((row_sum, row_squares), 'mp')  10.7 us
  transfers between devices with their start and end apart: 2, of which 1 were waited for; matrix products, arithmetic and copies ran while one was open for 0% of the time, Pallas kernels for 0%

commit v1 on v0

v1 whole, which is shorter than its diff:
```python
import functools
import math

import jax
import jax.numpy as jnp
from jax import lax
from jax.experimental import pallas as pl
from jax.experimental.pallas import tpu as pltpu
from jax.sharding import Mesh
from jax.sharding import PartitionSpec as P

D = 1024
DH = 128
SEG = 512
NEW = 64
USERS = 4
NZ = 16
NX = 4
NC = 2
XC = NX * NC
MP = 4
MB = 8
SEG_DEV = 2
W = D // MP
HEADS = W // DH
ZROWS = NZ * MB
FRESH = 16
PAY = ZROWS + SEG_DEV * FRESH
SCALE = 1.0 / math.sqrt(DH)
LOG2E = 1.4426950408889634
BF = jnp.bfloat16
F32 = jnp.float32

VMEM = pltpu.VMEM
SMEM = pltpu.SMEM


def vspec():
    return pl.BlockSpec(memory_space=VMEM)


def sspec():
    return pl.BlockSpec(memory_space=SMEM)


def project_kernel(cand, act, wq, wk, wv, out, rows):
    rows[...] = jnp.zeros_like(rows)
    rows[0:8] = jnp.dot(cand[...], wq[...], preferred_element_type=F32)
    rows[8:10] = jnp.dot(act[...], wk[...], preferred_element_type=F32)
    rows[10:12] = jnp.dot(act[...], wv[...], preferred_element_type=F32)
    msg = rows[...].astype(BF)
    for i in range(NZ):
        out[i] = msg


def project(cand, act, wq, wk, wv):
    return pl.pallas_call(
        project_kernel,
        out_shape=jax.ShapeDtypeStruct((NZ, 16, W), BF),
        in_specs=[vspec()] * 5,
        out_specs=vspec(),
        scratch_shapes=[pltpu.VMEM((16, W), F32)],
        name="project",
    )(cand, act, wq, wk, wv)


def spread_kernel(col, arr, out):
    x = arr[...].astype(F32)
    q = x[:, 0:8].reshape(ZROWS, W).astype(BF)
    f = x[:, 8:16].reshape(ZROWS, W).astype(BF)
    lane = lax.broadcasted_iota(jnp.int32, (XC * SEG_DEV * FRESH, ZROWS), 1)
    hot = (lane == col[...]).astype(F32).astype(BF)
    sel = jnp.dot(hot, f, preferred_element_type=F32).astype(BF)
    for t in range(XC):
        out[t, 0:ZROWS] = q
        out[t, ZROWS:PAY] = sel[t * 32 : t * 32 + 32]


def spread(col, arr):
    return pl.pallas_call(
        spread_kernel,
        out_shape=jax.ShapeDtypeStruct((XC, PAY, W), BF),
        in_specs=[vspec()] * 2,
        out_specs=vspec(),
        name="spread",
    )(col, arr)


def attend_kernel(info, maskrow, arr, keys, vals, part, new_keys, new_vals, acc):
    s = pl.program_id(0)
    length = info[s, 0]
    added = info[s, 1]
    fresh = arr[:, pl.ds(pl.multiple_of(ZROWS + s * FRESH, FRESH), FRESH), :]
    fresh = fresh.reshape(XC * FRESH, W)
    pos = lax.broadcasted_iota(jnp.int32, (SEG, XC * FRESH), 0) - length
    j = lax.broadcasted_iota(jnp.int32, (SEG, XC * FRESH), 1)
    k = j % 4
    step = ((j // 4) % 4) * 16 + (j // 16) * 2
    rowpos = lax.broadcasted_iota(jnp.int32, (SEG, W), 0)
    fill = (rowpos >= length) & (rowpos < length + added)
    live = rowpos < length + added
    hot_k = ((pos == step + k) & (k < 2)).astype(F32).astype(BF)
    hot_v = ((pos == step + k - 2) & (k >= 2)).astype(F32).astype(BF)
    kk = jnp.where(
        fill, jnp.dot(hot_k, fresh, preferred_element_type=F32), keys[...].astype(F32)
    ).astype(BF)
    vv = jnp.where(
        fill, jnp.dot(hot_v, fresh, preferred_element_type=F32), vals[...].astype(F32)
    )
    new_keys[...] = kk
    new_vals[...] = vv.astype(BF)
    vz = jnp.where(live, vv, 0.0).astype(BF)
    row = lax.broadcasted_iota(jnp.int32, (XC * ZROWS, NZ * XC), 0)
    lane = lax.broadcasted_iota(jnp.int32, (XC * ZROWS, NZ * XC), 1)
    batch = ((row // MB) % NZ) * XC + row // ZROWS
    hot_b = (lane == batch).astype(F32).astype(BF)
    use = lax.dot_general(
        hot_b, maskrow[s], (((1,), (1,)), ((), ())), preferred_element_type=F32
    )
    for t in range(XC):
        lo = t * ZROWS
        use_t = use[lo : lo + ZROWS, 0:1]
        for h in range(HEADS):
            cs = slice(h * DH, (h + 1) * DH)
            logits = lax.dot_general(
                arr[t, 0:ZROWS, cs],
                kk[:, cs],
                (((1,), (1,)), ((), ())),
                preferred_element_type=F32,
            )
            e = jnp.exp2(logits * (-SCALE * LOG2E))
            wt = ((logits * SCALE) * pl.reciprocal(1.0 + e, approx=True)).astype(BF)
            o = jnp.dot(wt, vz[:, cs], preferred_element_type=F32) * use_t

            @pl.when(s == 0)
            def _():
                acc[lo : lo + ZROWS, cs] = o

            @pl.when(s == 1)
            def _():
                part[t, :, cs] = (acc[lo : lo + ZROWS, cs] + o).astype(BF)


def attend(info, maskrow, arr, keys, vals):
    rows = SEG_DEV * SEG
    return pl.pallas_call(
        attend_kernel,
        grid=(SEG_DEV,),
        out_shape=(
            jax.ShapeDtypeStruct((XC, ZROWS, W), BF),
            jax.ShapeDtypeStruct((rows, W), BF),
            jax.ShapeDtypeStruct((rows, W), BF),
        ),
        in_specs=[
            sspec(),
            pl.BlockSpec((SEG_DEV, 8, NZ * XC), lambda s: (0, 0, 0)),
            pl.BlockSpec((XC, PAY, W), lambda s: (0, 0, 0)),
            pl.BlockSpec((SEG, W), lambda s: (s, 0)),
            pl.BlockSpec((SEG, W), lambda s: (s, 0)),
        ],
        out_specs=(
            pl.BlockSpec((XC, ZROWS, W), lambda s: (0, 0, 0)),
            pl.BlockSpec((SEG, W), lambda s: (s, 0)),
            pl.BlockSpec((SEG, W), lambda s: (s, 0)),
        ),
        scratch_shapes=[pltpu.VMEM((XC * ZROWS, W), F32)],
        compiler_params=pltpu.CompilerParams(vmem_limit_bytes=32 * 1024 * 1024),
        name="attend",
    )(info, maskrow, arr, keys, vals)


def fold_kernel(arr, out):
    out[...] = jnp.sum(arr[...].astype(F32), axis=0).astype(BF)


def fold(arr):
    return pl.pallas_call(
        fold_kernel,
        out_shape=jax.ShapeDtypeStruct((ZROWS, W), BF),
        in_specs=[vspec()],
        out_specs=vspec(),
        name="fold",
    )(arr)


def two_terms(x):
    hi = x.astype(BF)
    lo = (x - hi.astype(F32)).astype(BF)
    return hi, lo


def gate_kernel(cand, wg, wo, gate, base):
    v = jnp.dot(cand[...], wg[...], preferred_element_type=F32)
    g = v / (1.0 + jnp.exp(-v))
    gate[...] = g
    hi, lo = two_terms(g)
    base[...] = jnp.dot(hi, wo[...], preferred_element_type=F32) + jnp.dot(
        lo, wo[...], preferred_element_type=F32
    )


def gate_and_base(cand, wg, wo):
    return pl.pallas_call(
        gate_kernel,
        out_shape=(
            jax.ShapeDtypeStruct((MB, W), F32),
            jax.ShapeDtypeStruct((MB, D), F32),
        ),
        in_specs=[vspec()] * 3,
        out_specs=(vspec(), vspec()),
        name="gate",
    )(cand, wg, wo)


MSG = 2 * W + 128


def mix_kernel(arr, gate, base, wo, out):
    att = jnp.sum(arr[...].astype(F32).reshape(NZ, MB, W), axis=0)
    mean = jnp.sum(att, axis=1, keepdims=True) * (1.0 / W)
    d = att - mean
    sq = jnp.sum(d * d, axis=1, keepdims=True)
    hi, lo = two_terms(d * gate[...])
    a = jnp.dot(hi, wo[...], preferred_element_type=F32) + jnp.dot(
        lo, wo[...], preferred_element_type=F32
    )
    b = base[...]
    lane = lax.broadcasted_iota(jnp.int32, (MB, 128), 1)
    stats = jnp.where(lane == 0, mean, sq)
    for i in range(MP):
        out[i, :, 0:W] = a[:, i * W : (i + 1) * W]
        out[i, :, W : 2 * W] = b[:, i * W : (i + 1) * W]
        out[i, :, 2 * W : MSG] = stats


def mix(arr, gate, base, wo):
    return pl.pallas_call(
        mix_kernel,
        out_shape=jax.ShapeDtypeStruct((MP, MB, MSG), F32),
        in_specs=[vspec()] * 4,
        out_specs=vspec(),
        name="mix",
    )(arr, gate, base, wo)


def finish_kernel(me, arr, cand, out):
    means = [arr[i, :, 2 * W : 2 * W + 1] for i in range(MP)]
    mean = sum(means) * (1.0 / MP)
    square = sum(arr[i, :, 2 * W + 1 : 2 * W + 2] for i in range(MP))
    square = square + W * sum((m - mean) * (m - mean) for m in means)
    scale = lax.rsqrt(square * (1.0 / D) + 1e-05)
    total = sum(
        arr[i, :, 0:W] + (means[i] - mean) * arr[i, :, W : 2 * W] for i in range(MP)
    )
    own = cand[:, pl.ds(pl.multiple_of(me[0] * W, W), W)].astype(F32)
    out[...] = (own + total * scale).astype(BF)


def finish(me, arr, cand):
    return pl.pallas_call(
        finish_kernel,
        out_shape=jax.ShapeDtypeStruct((MB, W), BF),
        in_specs=[sspec(), vspec(), vspec()],
        out_specs=vspec(),
        name="finish",
    )(me, arr, cand)


def exchange(x, axes):
    return lax.all_to_all(x, axes, split_axis=0, concat_axis=0, tiled=True)


def per_device(
    candidates,
    actions,
    hist_keys,
    hist_values,
    w_query,
    w_gate,
    w_key,
    w_value,
    w_out,
    segment_list,
    segment_count,
    segment_length,
    new_count,
    batch_user,
):
    z = lax.axis_index("z")
    device = z * XC + lax.axis_index("x") * NC + lax.axis_index("core")
    me = lax.axis_index("mp").astype(jnp.int32).reshape(1)
    user_ids = jnp.arange(USERS, dtype=jnp.int32)
    slots = jnp.arange(segment_list.shape[1], dtype=jnp.int32)
    last_segment = jnp.sum(
        jnp.where(slots[None, :] == (segment_count - 1)[:, None], segment_list, 0), axis=1
    )

    rows = jnp.arange(XC * SEG_DEV * FRESH, dtype=jnp.int32)
    row_seg = z * XC * SEG_DEV + rows // FRESH
    row_hot = row_seg[:, None] == last_segment[None, :]
    row_user = jnp.sum(jnp.where(row_hot, user_ids[None, :], 0), axis=1)
    row_col = (row_user * 4 + (rows // 4) % 4) * 8 + rows % 4
    row_col = jnp.where(jnp.any(row_hot, axis=1), row_col, -1)[:, None]

    own = device * SEG_DEV + jnp.arange(SEG_DEV, dtype=jnp.int32)
    own_hot = own[:, None] == last_segment[None, :]
    own_added = jnp.sum(jnp.where(own_hot, new_count[None, :], 0), axis=1)
    own_length = lax.dynamic_slice_in_dim(segment_length, device * SEG_DEV, SEG_DEV)
    info = jnp.stack([own_length, own_added], axis=1)
    listed = jnp.any(segment_list[None, :, :] == own[:, None, None], axis=2)
    owner = jnp.sum(jnp.where(listed, user_ids[None, :], 0), axis=1)
    mask = (batch_user[None, :] == owner[:, None]).astype(BF)
    mask = jnp.broadcast_to(mask[:, None, :], (SEG_DEV, 8, NZ * XC))

    with jax.named_scope("gather"):
        message = project(candidates, actions, w_query, w_key, w_value)
        arrived = exchange(message, "z")
        payload = spread(row_col, arrived)
        queries = exchange(payload, ("x", "core"))
    gate, base = gate_and_base(candidates, w_gate, w_out)
    with jax.named_scope("attend"):
        part, new_keys, new_values = attend(info, mask, queries, hist_keys, hist_values)
    with jax.named_scope("return"):
        part = exchange(part, ("x", "core"))
        part = fold(part)
        part = exchange(part, "z")
    with jax.named_scope("mix"):
        mixed = mix(part, gate, base, w_out)
        mixed = exchange(mixed, "mp")
        ranked = finish(me, mixed, candidates)
    return (ranked, new_keys, new_values)


def solution(mesh):
    names = ("z", "x", "core", "mp")
    inner = Mesh(mesh.devices.reshape(NZ, NX, NC, MP), names)
    hist = ("z", "x", "core")
    in_specs = (
        P(hist, None),
        P(hist, None),
        P(hist, "mp"),
        P(hist, "mp"),
        P(None, "mp"),
        P(None, "mp"),
        P(None, "mp"),
        P(None, "mp"),
        P("mp", None),
        P(),
        P(),
        P(),
        P(),
        P(),
    )
    out_specs = (P(hist, "mp"), P(hist, "mp"), P(hist, "mp"))
    return jax.shard_map(
        per_device, mesh=inner, in_specs=in_specs, out_specs=out_specs, check_vma=False
    )
```

time: 293 us -> 112 us (0.38)
  blocking collectives: 210 us -> 13.5 us
  Pallas kernels: 0 us -> 25.9 us
  waiting for transfers between devices: 20.8 us -> 35.8 us
  between operations: 14.3 us -> 0.73 us
  matrix products: 9.37 us -> 0 us
  starting transfers between devices: 19.4 us -> 28.4 us
  other arithmetic: 9.87 us -> 1.79 us
  local copies, waits for them, and re-layouts: 8.08 us -> 4.74 us
    all_to_all x1, blocking collectives: 111 us -> 13.5 us  [exchange(): return lax.all_to_all(x, axes, split_axis=0, concat_axis=0, tiled=True)]
    all_gather x1 -> x0, blocking collectives: 87.9 us -> none  [per_device(): query_piece = lax.all_gather(queries, 'hist', axis=0, tiled=True)]
    all_to_all x1 -> x4, waiting for transfers between devices: 0.01 us -> 35.8 us  [exchange(): return lax.all_to_all(x, axes, split_axis=0, concat_axis=0, tiled=True)]
    pallas_call x0 -> x7, Pallas kernels: none -> 25.9 us  [the longest x1 13.6 us: attend(): pl.pallas_call(attend_kernel, grid=(SEG_DEV,), out_shape=(jax.ShapeDtypeS...]
    reduce_scatter x1 -> x0, waiting for transfers between devices: 20.8 us -> none  [per_device(): lax.psum_scatter(out_terms, 'mp', scatter_dimension=1, tiled=True)]
    psum x1 -> x0, blocking collectives: 10.7 us -> none  [per_device(): row_sum, row_squares = lax.psum((row_sum, row_squares), 'mp')]
    dot_general x12 -> x0, matrix products: 9.37 us -> none  [the longest x4 4.46 us: score_block(): jnp.einsum('lne,eli->nli', attention_weight, segment_value_rows[segment_p...]
    all_to_all x1 -> x4, starting transfers between devices: 19.4 us -> 28.4 us  [exchange(): return lax.all_to_all(x, axes, split_axis=0, concat_axis=0, tiled=True)]
  transfers between devices with their start and end apart: 2 -> 4, of which waited for: 1 -> 4; matrix products, arithmetic and copies ran while one was open for 0% -> 2% of each run, Pallas kernels for 0% -> 2%
where the time goes in v1:
time: 112 us; the launch traced here: 111 us
  waiting for transfers between devices  35.8 us (32%)
  starting transfers between devices  28.4 us (25%)
  Pallas kernels  25.9 us (23%)
  blocking collectives  13.5 us (12%)
  local copies, waits for them, and re-layouts  4.74 us (4%)
  other arithmetic  1.79 us (2%)
    all_to_all x4, waiting for transfers between devices, exchange(): return lax.all_to_all(x, axes, split_axis=0, concat_axis=0, tiled=True)  35.8 us
    all_to_all x4, starting transfers between devices, exchange(): return lax.all_to_all(x, axes, split_axis=0, concat_axis=0, tiled=True)  28.4 us
    pallas_call x1, Pallas kernels, attend(): pl.pallas_call(attend_kernel, grid=(SEG_DEV,), out_shape=(jax.ShapeDtypeS...  13.6 us
    all_to_all x1, blocking collectives, exchange(): return lax.all_to_all(x, axes, split_axis=0, concat_axis=0, tiled=True)  13.5 us
    unnamed x20, local copies, waits for them, and re-layouts  4.34 us
    pallas_call x1, Pallas kernels, project(): pl.pallas_call(project_kernel, out_shape=jax.ShapeDtypeStruct((NZ, 16, W)...  2.38 us
    pallas_call x1, Pallas kernels, gate_and_base(): pl.pallas_call(gate_kernel, out_shape=(jax.ShapeDtypeStruct((MB, W), F32)...  2.37 us
  transfers between devices with their start and end apart: 4, of which 4 were waited for; matrix products, arithmetic and copies ran while one was open for 2% of the time, Pallas kernels for 2%

profile of v1, /device:TPU:6, one launch (start us, length us, event | category | flops | bytes accessed | tf_op | source)
XLA Modules:
  0.0 110.8 jit_solution(9806098178506111995)
XLA Ops:
  0.6 0.0 copy-start
  0.6 2.4 %project.1 = bf16[16,16,256]{2,1,0:T(8,128)(2,1)} custom-call(bf16[8,1024]{1,0:T(8,128)(2,1)} %cand.5, bf16[2,1024]{1,0:T(2,128)(2,1)} %act.1, bf16[1024,256]{1,0:T(8,128)(2,1)} %wq.1, bf16[1024,256]{1,0:T(8,128)(2,1)} %wk.1, bf16[1024,256]{1,0:T(8,128)(2,1)} %wv.1), custom_call_target="tpu_custom_call" | custom-call | tf_op jit(solution)/shard_map/gather/project/pallas_call | solution.py:57
  3.0 15.2 %all-to-all-start = ((bf16[16,16,256]{2,1,0:T(8,128)(2,1)}), bf16[16,16,256]{2,1,0:T(8,128)(2,1)S(1)}, u32[]{:S(2)}, u32[]{:S(2)}) async-start(bf16[16,16,256]{2,1,0:T(8,128)(2,1)} %project.1), calls=%async_computation | async-start | bytes 262144 | tf_op jit(solution)/shard_map/gather/all_to_all | solution.py:270
  18.2 0.0 copy-start.8
  18.3 0.6 copy-done.8
  18.9 0.0 copy-start.6
  18.9 0.7 copy-done.6
  19.6 0.2 select_reduce_fusion
  19.8 0.1 fusion.9
  19.9 0.1 copy.25
  20.0 0.0 copy-start.7
  20.0 0.1 compare_reduce_fusion
  20.1 0.6 copy-done.7
  20.7 0.2 fusion.10
  20.9 0.8 fusion.8.col
  21.6 11.3 %all-to-all-done.arr = bf16[16,16,256]{2,1,0:T(8,128)(2,1)S(1)} async-done(((bf16[16,16,256]{2,1,0:T(8,128)(2,1)}), bf16[16,16,256]{2,1,0:T(8,128)(2,1)S(1)}, u32[]{:S(2)}, u32[]{:S(2)}) %all-to-all-start) | async-done | bytes 131104 | tf_op jit(solution)/shard_map/gather/all_to_all | solution.py:270
  32.9 0.0 copy-start.3
  32.9 0.7 copy-done.3
  33.6 2.0 %spread.1 = bf16[8,160,256]{2,1,0:T(8,128)(2,1)} custom-call(s32[256,1]{1,0:T(8,128)} %fusion.8.col, bf16[16,16,256]{2,1,0:T(8,128)(2,1)} %copy-done.3), custom_call_target="tpu_custom_call" | custom-call | tf_op jit(solution)/shard_map/gather/spread/pallas_call | solution.py:80
  35.6 0.0 copy-start.1
  35.6 0.0 copy-start.2
  35.6 4.9 %all-to-all-start.1 = ((bf16[8,160,256]{2,1,0:T(8,128)(2,1)}), bf16[8,160,256]{2,1,0:T(8,128)(2,1)S(1)}, u32[]{:S(2)}, u32[]{:S(2)}) async-start(bf16[8,160,256]{2,1,0:T(8,128)(2,1)} %spread.1), calls=%async_computation.1 | async-start | bytes 1310720 | tf_op jit(solution)/shard_map/gather/all_to_all | solution.py:270
  40.5 0.0 copy-done
  40.5 0.1 dynamic-slice_bitcast_fusion
  40.6 0.1 copy.23
  40.7 0.1 copy.24
  40.8 0.1 pad_add_fusion.info
  40.9 0.2 compare_reduce_fusion.1
  41.1 0.0 copy-start.9
  41.1 0.1 select_reduce_fusion.1
  41.2 0.5 copy-done.9
  41.8 0.1 compare_convert_fusion
  41.8 8.4 %all-to-all-done.1.arr = bf16[8,160,256]{2,1,0:T(8,128)(2,1)S(1)} async-done(((bf16[8,160,256]{2,1,0:T(8,128)(2,1)}), bf16[8,160,256]{2,1,0:T(8,128)(2,1)S(1)}, u32[]{:S(2)}, u32[]{:S(2)}) %all-to-all-start.1) | async-done | bytes 655392 | tf_op jit(solution)/shard_map/gather/all_to_all | solution.py:270
  50.2 0.0 copy-done.1
  50.2 0.0 copy-done.2
  50.2 13.6 %attend.1 = (bf16[8,128,256]{2,1,0:T(8,128)(2,1)S(1)}, bf16[1024,256]{1,0:T(8,128)(2,1)}, bf16[1024,256]{1,0:T(8,128)(2,1)}) custom-call(s32[2,2]{1,0:T(2,128)S(1)} %pad_add_fusion.info, bf16[2,8,128]{2,1,0:T(8,128)(2,1)S(1)} %broadcast_in_dim.60.maskrow, bf16[8,160,256]{2,1,0:T(8,128)(2,1)S(1)} %all-to-all-done.1.arr, bf16[1024,256]{1,0:T(8,128)(2,1)S(1)} %copy-done.1, ...), custom_call_target="tpu_custom_call" | custom-call | tf_op jit(solution)/shard_map/attend/attend/pallas_call | solution.py:146
  63.9 13.5 %all_to_all.31.arr = bf16[8,128,256]{2,1,0:T(8,128)(2,1)} all-to-all(bf16[8,128,256]{2,1,0:T(8,128)(2,1)S(1)} %get-tuple-element.8), channel_id=1, replica_groups=mesh['z'=16,'x'=4,'core'=2,'mp'=4] {'x','core'}, dimensions={0} | all-to-all | bytes 1048576 | tf_op jit(solution)/shard_map/return/all_to_all | solution.py:270
  77.3 1.7 %fold.1 = bf16[128,256]{1,0:T(8,128)(2,1)} custom-call(bf16[8,128,256]{2,1,0:T(8,128)(2,1)} %all_to_all.31.arr), custom_call_target="tpu_custom_call" | custom-call | tf_op jit(solution)/shard_map/return/fold/pallas_call | solution.py:177
  79.1 3.8 %all-to-all-start.3 = ((bf16[16,8,256]{2,1,0:T(8,128)(2,1)}), bf16[16,8,256]{2,1,0:T(8,128)(2,1)S(1)}, u32[]{:S(2)}, u32[]{:S(2)}) async-start(bf16[16,8,256]{2,1,0:T(8,128)(2,1)} %bitcast.7), calls=%async_computation.3 | async-start | bytes 131072 | tf_op jit(solution)/shard_map/return/all_to_all | solution.py:270
  82.9 2.4 %gate.1 = (f32[8,256]{1,0:T(8,128)}, f32[8,1024]{1,0:T(8,128)}) custom-call(bf16[8,1024]{1,0:T(8,128)(2,1)} %cand.5, bf16[1024,256]{1,0:T(8,128)(2,1)} %wg.1, bf16[256,1024]{1,0:T(8,128)(2,1)} %wo.3), custom_call_target="tpu_custom_call" | custom-call | tf_op jit(solution)/shard_map/gate/pallas_call | solution.py:203
  85.3 10.4 %all-to-all-done.3 = bf16[16,8,256]{2,1,0:T(8,128)(2,1)S(1)} async-done(((bf16[16,8,256]{2,1,0:T(8,128)(2,1)}), bf16[16,8,256]{2,1,0:T(8,128)(2,1)S(1)}, u32[]{:S(2)}, u32[]{:S(2)}) %all-to-all-start.3) | async-done | bytes 65568 | tf_op jit(solution)/shard_map/return/all_to_all | solution.py:270
  95.7 0.0 copy-start.5
  95.7 0.6 copy-done.5
  96.3 2.1 %mix.1 = f32[4,8,640]{2,1,0:T(8,128)} custom-call(bf16[128,256]{1,0:T(8,128)(2,1)} %bitcast.8, f32[8,256]{1,0:T(8,128)} %get-tuple-element.9.gate, f32[8,1024]{1,0:T(8,128)} %get-tuple-element.10.base, bf16[256,1024]{1,0:T(8,128)(2,1)} %wo.3), custom_call_target="tpu_custom_call" | custom-call | tf_op jit(solution)/shard_map/mix/mix/pallas_call | solution.py:237
  98.4 4.5 %all-to-all-start.4 = ((f32[4,8,640]{2,1,0:T(8,128)}), f32[4,8,640]{2,1,0:T(8,128)S(1)}, u32[]{:S(2)}, u32[]{:S(2)}) async-start(f32[4,8,640]{2,1,0:T(8,128)} %mix.1), calls=%async_computation.4 | async-start | bytes 163840 | tf_op jit(solution)/shard_map/mix/all_to_all | solution.py:270
  102.8 5.7 %all-to-all-done.4.arr = f32[4,8,640]{2,1,0:T(8,128)S(1)} async-done(((f32[4,8,640]{2,1,0:T(8,128)}), f32[4,8,640]{2,1,0:T(8,128)S(1)}, u32[]{:S(2)}, u32[]{:S(2)}) %all-to-all-start.4) | async-done | bytes 81952 | tf_op jit(solution)/shard_map/mix/all_to_all | solution.py:270
  108.5 0.0 copy-start.4
  108.5 0.6 copy-done.4
  109.2 1.6 %finish.1 = bf16[8,256]{1,0:T(8,128)(2,1)} custom-call(s32[1]{0:T(128)} %bitcast.me, f32[4,8,640]{2,1,0:T(8,128)} %copy-done.4, bf16[8,1024]{1,0:T(8,128)(2,1)} %cand.5), custom_call_target="tpu_custom_call" | custom-call | tf_op jit(solution)/shard_map/mix/finish/pallas_call | solution.py:260
  (5 shorter events, 0.0 us)
Async XLA Ops:
  0.6 39.9 %copy-start = (s32[256]{0:T(256)S(1)}, s32[256]{0:T(256)}, u32[]{:S(2)}) copy-start(s32[256]{0:T(256)} %param.25) | copy-start | bytes 3076
  3.0 29.9 %all-to-all-start = ((bf16[16,16,256]{2,1,0:T(8,128)(2,1)}), bf16[16,16,256]{2,1,0:T(8,128)(2,1)S(1)}, u32[]{:S(2)}, u32[]{:S(2)}) async-start(bf16[16,16,256]{2,1,0:T(8,128)(2,1)} %project.1), calls=%async_computation | async-start | bytes 262144 | tf_op jit(solution)/shard_map/gather/all_to_all | solution.py:270
  18.2 0.7 copy-start.8
  18.9 0.7 copy-start.6
  20.0 0.7 copy-start.7
  32.9 0.7 copy-start.3
  35.6 14.6 %copy-start.1 = (bf16[1024,256]{1,0:T(8,128)(2,1)S(1)}, bf16[1024,256]{1,0:T(8,128)(2,1)}, u32[]{:S(2)}) copy-start(bf16[1024,256]{1,0:T(8,128)(2,1)} %keys.1) | copy-start | bytes 1572868
  35.6 14.6 %copy-start.2 = (bf16[1024,256]{1,0:T(8,128)(2,1)S(1)}, bf16[1024,256]{1,0:T(8,128)(2,1)}, u32[]{:S(2)}) copy-start(bf16[1024,256]{1,0:T(8,128)(2,1)} %vals.1) | copy-start | bytes 1572868
  35.6 14.6 %all-to-all-start.1 = ((bf16[8,160,256]{2,1,0:T(8,128)(2,1)}), bf16[8,160,256]{2,1,0:T(8,128)(2,1)S(1)}, u32[]{:S(2)}, u32[]{:S(2)}) async-start(bf16[8,160,256]{2,1,0:T(8,128)(2,1)} %spread.1), calls=%async_computation.1 | async-start | bytes 1310720 | tf_op jit(solution)/shard_map/gather/all_to_all | solution.py:270
  41.1 0.7 copy-start.9
  79.1 16.6 %all-to-all-start.3 = ((bf16[16,8,256]{2,1,0:T(8,128)(2,1)}), bf16[16,8,256]{2,1,0:T(8,128)(2,1)S(1)}, u32[]{:S(2)}, u32[]{:S(2)}) async-start(bf16[16,8,256]{2,1,0:T(8,128)(2,1)} %bitcast.7), calls=%async_computation.3 | async-start | bytes 131072 | tf_op jit(solution)/shard_map/return/all_to_all | solution.py:270
  95.7 0.6 copy-start.5
  98.4 10.2 %all-to-all-start.4 = ((f32[4,8,640]{2,1,0:T(8,128)}), f32[4,8,640]{2,1,0:T(8,128)S(1)}, u32[]{:S(2)}, u32[]{:S(2)}) async-start(f32[4,8,640]{2,1,0:T(8,128)} %mix.1), calls=%async_computation.4 | async-start | bytes 163840 | tf_op jit(solution)/shard_map/mix/all_to_all | solution.py:270
  108.5 0.6 copy-start.4

commit v2 on v1

v2 whole, which is shorter than its diff:
```python
import functools
import math

import jax
import jax.numpy as jnp
from jax import lax
from jax.experimental import pallas as pl
from jax.experimental.pallas import tpu as pltpu
from jax.sharding import Mesh
from jax.sharding import PartitionSpec as P

D = 1024
DH = 128
SEG = 512
NEW = 64
USERS = 4
NZ = 16
NX = 4
NC = 2
XC = NX * NC
ZX = NZ * NX
MP = 4
MB = 8
SEG_DEV = 2
W = D // MP
HEADS = W // DH
BATCHES = NZ * XC
QROWS = BATCHES * MB
HALF = ZX * MB
ZROWS = NZ * MB
FIRST_Z = 12
ACT = 2
SCALE = 1.0 / math.sqrt(DH)
LOG2E = 1.4426950408889634
BF = jnp.bfloat16
F32 = jnp.float32
MIB = 1024 * 1024


def vspec():
    return pl.BlockSpec(memory_space=pltpu.VMEM)


def sspec():
    return pl.BlockSpec(memory_space=pltpu.SMEM)


def aspec():
    return pl.BlockSpec(memory_space=pl.ANY)


def params(mib):
    return pltpu.CompilerParams(vmem_limit_bytes=mib * MIB)


def cost(flops, nbytes):
    return pl.CostEstimate(flops=flops, bytes_accessed=nbytes, transcendentals=0)


def project_kernel(cand, act, wq, wk, wv, msg, kx, vx, c, a, q, k, v, block, sems):
    pairs = ((cand, c), (wq, q), (act, a), (wk, k), (wv, v))
    copies = [pltpu.make_async_copy(x, y, sems.at[i]) for i, (x, y) in enumerate(pairs)]
    for copy in copies:
        copy.start()
    block[...] = jnp.zeros_like(block)
    copies[0].wait()
    copies[1].wait()
    query = jnp.dot(c[...], q[...], preferred_element_type=F32).astype(BF)
    copies[2].wait()
    copies[3].wait()
    key = jnp.dot(a[...], k[...], preferred_element_type=F32)
    copies[4].wait()
    value = jnp.dot(a[...], v[...], preferred_element_type=F32)
    for h in range(HEADS):
        cs = slice(h * DH, (h + 1) * DH)
        block[h * 4 : h * 4 + 2, 0:DH] = key[:, cs]
        block[h * 4 + 2 : h * 4 + 4, 0:DH] = value[:, cs]
    fresh = block[0:MB, 0:DH].astype(BF)
    for i in range(NZ):
        msg[i, :, 0:W] = query
        msg[i, :, W : W + DH] = fresh
    block[0:MB, 0:DH] = jnp.zeros((MB, DH), F32)
    lane = lax.broadcasted_iota(jnp.int32, (ACT, W), 1)
    for src, dst in ((key, kx), (value, vx)):
        for h in range(HEADS):
            block[h * ACT : (h + 1) * ACT] = jnp.where(lane // DH == h, src, 0.0)
        dst[...] = block[...].astype(BF)


def project(cand, act, wq, wk, wv):
    weight = pltpu.VMEM((D, W), BF)
    return pl.pallas_call(
        project_kernel,
        out_shape=(
            jax.ShapeDtypeStruct((NZ, MB, W + DH), BF),
            jax.ShapeDtypeStruct((DH, W), BF),
            jax.ShapeDtypeStruct((DH, W), BF),
        ),
        in_specs=[aspec()] * 5,
        out_specs=(vspec(),) * 3,
        scratch_shapes=[
            pltpu.VMEM((MB, D), BF),
            pltpu.VMEM((ACT, D), BF),
            weight,
            weight,
            weight,
            pltpu.VMEM((DH, W), F32),
            pltpu.SemaphoreType.DMA((5,)),
        ],
        name="project",
    )(cand, act, wq, wk, wv)


def spread_kernel(arr, out):
    rows = arr[...]
    for t in range(NX):
        out[t] = rows


def spread(arr):
    return pl.pallas_call(
        spread_kernel,
        out_shape=jax.ShapeDtypeStruct((NX, ZROWS, W + DH), BF),
        in_specs=[vspec()],
        out_specs=vspec(),
        compiler_params=params(8),
        name="spread",
    )(arr)


BLOCK = 512
PATCH = NEW + 16


def attend_kernel(
    info, maskrow, arr, kx, vx, keys, vals, part, new_keys, new_vals, patch, sems
):
    pairs = ((keys, new_keys), (vals, new_vals))
    copies = [pltpu.make_async_copy(x, y, sems.at[i]) for i, (x, y) in enumerate(pairs)]
    for copy in copies:
        copy.start()

    shape = (PATCH, XC * 4 * MB)
    j = lax.broadcasted_iota(jnp.int32, shape, 1)
    source = ((j // 32) % NX) * NC + j // 128
    step = ((j // 8) % 4) * 16 + source * 2 + j % 2
    kind = (j // 2) % 4
    patches = []
    for s in range(SEG_DEV):
        length = info[s, 0]
        added = info[s, 1]
        start = ((info[s, 2] * 4 + (NZ - FIRST_Z)) % NZ) * MB
        begin = pl.multiple_of(jnp.minimum((length // 16) * 16, SEG - PATCH), 16)
        fresh = arr[:, pl.ds(pl.multiple_of(start, 4 * MB), 4 * MB), W : W + DH]
        fresh = fresh.reshape(XC * 4 * MB, DH)
        pos = lax.broadcasted_iota(jnp.int32, shape, 0) + (begin - length)
        rowpos = lax.broadcasted_iota(jnp.int32, (PATCH, DH), 0) + (begin - length)
        fill = (rowpos >= 0) & (rowpos < added)
        rows = pl.ds(pl.multiple_of(s * SEG + begin, 16), PATCH)
        for i, (old, new) in enumerate(pairs):
            slot = s * 2 + i
            for h in range(HEADS):
                cs = slice(h * DH, (h + 1) * DH)
                hot = ((pos == step) & (kind == 2 * h + i)).astype(F32).astype(BF)
                placed = jnp.dot(hot, fresh, preferred_element_type=F32)
                kept = old[rows, cs].astype(F32)
                patch[slot, :, cs] = jnp.where(fill, placed, kept).astype(BF)
            patches.append(
                pltpu.make_async_copy(patch.at[slot], new.at[rows], sems.at[2 + slot])
            )

    row = lax.broadcasted_iota(jnp.int32, (QROWS, BATCHES), 0)
    lane = lax.broadcasted_iota(jnp.int32, (QROWS, BATCHES), 1)
    step = (row % ZROWS) // MB
    group = row // ZROWS
    batch = ((step + FIRST_Z) % NZ) * XC + (group % NX) * NC + group // NX
    hot = (lane == batch).astype(F32).astype(BF)
    use = lax.dot_general(
        hot, maskrow[...], (((1,), (1,)), ((), ())), preferred_element_type=F32
    )
    rowpos = lax.broadcasted_iota(jnp.int32, (SEG, W), 0)
    zero = jnp.zeros((), BF)
    live = []
    for s in range(SEG_DEV):
        v = vals[s * SEG : (s + 1) * SEG].astype(F32)
        live.append(jnp.where(rowpos < info[s, 0], v, 0.0).astype(BF))

    fresh = lax.broadcasted_iota(jnp.int32, (DH, W), 0) % ACT
    own = jnp.where(fresh < info[SEG_DEV, 0], vx[...].astype(F32), 0.0).astype(BF)

    def weigh(logits):
        e = jnp.exp2(logits * (-SCALE * LOG2E))
        return ((logits * SCALE) * pl.reciprocal(1.0 + e, approx=True)).astype(BF)

    def score(a, b):
        return lax.dot_general(a, b, (((1,), (1,)), ((), ())), preferred_element_type=F32)

    for r in range(0, QROWS, BLOCK):
        if r == BLOCK:
            for copy in copies:
                copy.wait()
            for copy in patches:
                copy.start()
        first = r // ZROWS
        qr = arr[first : first + BLOCK // ZROWS, :, 0:W].reshape(BLOCK, W)
        wx = weigh(score(qr, kx[...]))
        ox = jnp.dot(wx, own, preferred_element_type=F32) * use[r : r + BLOCK, 2:3]
        for h in range(HEADS):
            cs = slice(h * DH, (h + 1) * DH)
            total = ox[:, cs]
            for s in range(SEG_DEV):
                wt = weigh(score(qr[:, cs], keys[s * SEG : (s + 1) * SEG, cs]))
                o = jnp.dot(wt, live[s][:, cs], preferred_element_type=F32)
                total = total + o * use[r : r + BLOCK, s : s + 1]
            total = total.astype(BF)
            for i in range(BLOCK // ZROWS):
                group = r // ZROWS + i
                lo = i * ZROWS
                part[(group % NX) * NC + group // NX, :, cs] = total[lo : lo + ZROWS]
    for copy in patches:
        copy.wait()


def attend(info, maskrow, arr, kx, vx, keys, vals):
    stored = jax.ShapeDtypeStruct((SEG_DEV * SEG, W), BF)
    return pl.pallas_call(
        attend_kernel,
        out_shape=(jax.ShapeDtypeStruct((XC, ZROWS, W), BF), stored, stored),
        in_specs=[sspec()] + [vspec()] * 6,
        out_specs=(vspec(), aspec(), aspec()),
        scratch_shapes=[
            pltpu.VMEM((SEG_DEV * 2, PATCH, W), BF),
            pltpu.SemaphoreType.DMA((2 + SEG_DEV * 2,)),
        ],
        compiler_params=params(32),
        name="attend",
    )(info, maskrow, arr, kx, vx, keys, vals)


def fold_kernel(arr, out):
    out[...] = jnp.sum(arr[...].astype(F32), axis=0).astype(BF)


def fold(arr):
    return pl.pallas_call(
        fold_kernel,
        out_shape=jax.ShapeDtypeStruct((ZROWS, W), BF),
        in_specs=[vspec()],
        out_specs=vspec(),
        compiler_params=params(8),
        name="fold",
    )(arr)


def two_terms(x):
    hi = x.astype(BF)
    lo = (x - hi.astype(F32)).astype(BF)
    return hi, lo


def gate_kernel(cand, wg, wo, gate, base):
    v = jnp.dot(cand[...], wg[...], preferred_element_type=F32)
    g = v / (1.0 + jnp.exp(-v))
    gate[...] = g
    hi, lo = two_terms(g)
    base[...] = jnp.dot(hi, wo[...], preferred_element_type=F32) + jnp.dot(
        lo, wo[...], preferred_element_type=F32
    )


def gate_and_base(cand, wg, wo):
    return pl.pallas_call(
        gate_kernel,
        out_shape=(
            jax.ShapeDtypeStruct((MB, W), F32),
            jax.ShapeDtypeStruct((MB, D), F32),
        ),
        in_specs=[vspec()] * 3,
        out_specs=(vspec(), vspec()),
        compiler_params=params(8),
        cost_estimate=cost(10_000_000, 1_200_000),
        name="gate",
    )(cand, wg, wo)


MSG = 2 * W + 128


def mix_kernel(arr, gate, base, wo, out):
    att = jnp.sum(arr[...].astype(F32).reshape(NZ, MB, W), axis=0)
    mean = jnp.sum(att, axis=1, keepdims=True) * (1.0 / W)
    d = att - mean
    sq = jnp.sum(d * d, axis=1, keepdims=True)
    hi, lo = two_terms(d * gate[...])
    a = jnp.dot(hi, wo[...], preferred_element_type=F32) + jnp.dot(
        lo, wo[...], preferred_element_type=F32
    )
    b = base[...]
    lane = lax.broadcasted_iota(jnp.int32, (MB, 128), 1)
    stats = jnp.where(lane == 0, mean, sq)
    for i in range(MP):
        out[i, :, 0:W] = a[:, i * W : (i + 1) * W]
        out[i, :, W : 2 * W] = b[:, i * W : (i + 1) * W]
        out[i, :, 2 * W : MSG] = stats


def mix(arr, gate, base, wo):
    return pl.pallas_call(
        mix_kernel,
        out_shape=jax.ShapeDtypeStruct((MP, MB, MSG), F32),
        in_specs=[vspec()] * 4,
        out_specs=vspec(),
        compiler_params=params(8),
        name="mix",
    )(arr, gate, base, wo)


def finish_kernel(me, arr, cand, out):
    means = [arr[i, :, 2 * W : 2 * W + 1] for i in range(MP)]
    mean = sum(means) * (1.0 / MP)
    square = sum(arr[i, :, 2 * W + 1 : 2 * W + 2] for i in range(MP))
    square = square + W * sum((m - mean) * (m - mean) for m in means)
    scale = lax.rsqrt(square * (1.0 / D) + 1e-05)
    total = sum(
        arr[i, :, 0:W] + (means[i] - mean) * arr[i, :, W : 2 * W] for i in range(MP)
    )
    own = cand[:, pl.ds(pl.multiple_of(me[0] * W, W), W)].astype(F32)
    out[...] = (own + total * scale).astype(BF)


def finish(me, arr, cand):
    return pl.pallas_call(
        finish_kernel,
        out_shape=jax.ShapeDtypeStruct((MB, W), BF),
        in_specs=[sspec(), vspec(), vspec()],
        out_specs=vspec(),
        compiler_params=params(8),
        name="finish",
    )(me, arr, cand)


def exchange(x, axes):
    groups = [[(i + FIRST_Z) % NZ for i in range(NZ)]] if axes == "z" else None
    return lax.all_to_all(
        x, axes, split_axis=0, concat_axis=0, tiled=True, axis_index_groups=groups
    )


def per_device(
    candidates,
    actions,
    hist_keys,
    hist_values,
    w_query,
    w_gate,
    w_key,
    w_value,
    w_out,
    segment_list,
    segment_count,
    segment_length,
    new_count,
    batch_user,
):
    z = lax.axis_index("z").astype(jnp.int32)
    core = lax.axis_index("core").astype(jnp.int32)
    device = z * XC + lax.axis_index("x").astype(jnp.int32) * NC + core
    me = lax.axis_index("mp").astype(jnp.int32).reshape(1)
    user_ids = jnp.arange(USERS, dtype=jnp.int32)
    slots = jnp.arange(segment_list.shape[1], dtype=jnp.int32)
    last_segment = jnp.sum(
        jnp.where(slots[None, :] == (segment_count - 1)[:, None], segment_list, 0), axis=1
    )

    own = device * SEG_DEV + jnp.arange(SEG_DEV, dtype=jnp.int32)
    own_hot = own[:, None] == last_segment[None, :]
    own_added = jnp.sum(jnp.where(own_hot, new_count[None, :], 0), axis=1)
    own_user = jnp.sum(jnp.where(own_hot, user_ids[None, :], 0), axis=1)
    own_length = lax.dynamic_slice_in_dim(segment_length, device * SEG_DEV, SEG_DEV)
    listed = jnp.any(segment_list[None, :, :] == own[:, None, None], axis=2)
    owner = jnp.sum(jnp.where(listed, user_ids[None, :], 0), axis=1)

    act_user = device * ACT // NEW
    act_count = jnp.sum(jnp.where(user_ids == act_user, new_count, 0))
    act_valid = jnp.clip(act_count - device * ACT % NEW, 0, ACT)
    nothing = jnp.zeros((), jnp.int32)
    info = jnp.stack(
        [
            jnp.append(own_length, act_valid),
            jnp.append(own_added, nothing),
            jnp.append(own_user, nothing),
        ],
        axis=1,
    )
    mask_user = jnp.concatenate([owner, jnp.broadcast_to(act_user, (6,))])
    mask = (batch_user[None, :] == mask_user[:, None]).astype(BF)

    with jax.named_scope("gather"):
        message, key_block, value_block = project(
            candidates, actions, w_query, w_key, w_value
        )
        arrived = exchange(message, "z")
        gate, base = gate_and_base(candidates, w_gate, w_out)
        arrived, gate, base, info, mask, me = lax.optimization_barrier(
            (arrived, gate, base, info, mask, me)
        )
        arrived = exchange(spread(arrived.reshape(ZROWS, W + DH)), "x")
        arrived = lax.all_gather(arrived, "core", axis=0)
    with jax.named_scope("attend"):
        part, new_keys, new_values = attend(
            info,
            mask,
            arrived.reshape(XC, ZROWS, W + DH),
            key_block,
            value_block,
            hist_keys,
            hist_values,
        )
    with jax.named_scope("return"):
        part = fold(exchange(part, ("x", "core")))
        summed = exchange(part, "z")
    with jax.named_scope("mix"):
        mixed = mix(summed, gate, base, w_out)
        mixed = exchange(mixed, "mp")
        ranked = finish(me, mixed, candidates)
    return (ranked, new_keys, new_values)


def solution(mesh):
    names = ("z", "x", "core", "mp")
    inner = Mesh(mesh.devices.reshape(NZ, NX, NC, MP), names)
    hist = ("z", "x", "core")
    in_specs = (
        P(hist, None),
        P(hist, None),
        P(hist, "mp"),
        P(hist, "mp"),
        P(None, "mp"),
        P(None, "mp"),
        P(None, "mp"),
        P(None, "mp"),
        P("mp", None),
        P(),
        P(),
        P(),
        P(),
        P(),
    )
    out_specs = (P(hist, "mp"), P(hist, "mp"), P(hist, "mp"))
    return jax.shard_map(
        per_device, mesh=inner, in_specs=in_specs, out_specs=out_specs, check_vma=False
    )
```

time: 112 us -> 86.2 us (0.77)
  blocking collectives: 13.5 us -> 51 us
  waiting for transfers between devices: 35.8 us -> 4.45 us
  Pallas kernels: 25.9 us -> 8.62 us
  starting transfers between devices: 28.4 us -> 15.7 us
  local copies, waits for them, and re-layouts: 4.74 us -> 2.28 us
    all_to_all x1 -> x4, blocking collectives: 13.5 us -> 48.5 us  [exchange(): lax.all_to_all(x, axes, split_axis=0, concat_axis=0, tiled=True, axis_ind...]
    all_to_all x4 -> x1, waiting for transfers between devices: 35.8 us -> 4.45 us  [exchange(): lax.all_to_all(x, axes, split_axis=0, concat_axis=0, tiled=True, axis_ind...]
    all_to_all x4 -> x1, starting transfers between devices: 28.4 us -> 15.7 us  [exchange(): lax.all_to_all(x, axes, split_axis=0, concat_axis=0, tiled=True, axis_ind...]
    pallas_call x3, Pallas kernels: 18.1 us -> 6.96 us  [the longest x1 4.37 us: attend(): pl.pallas_call(attend_kernel, out_shape=(jax.ShapeDtypeStruct((XC, ZROWS,...]
    all_gather x0 -> x1, blocking collectives: none -> 2.5 us  [per_device(): arrived = lax.all_gather(arrived, 'core', axis=0)]
    unnamed x20 -> x24, local copies, waits for them, and re-layouts: 4.34 us -> 1.93 us
    pallas_call x1, Pallas kernels: 2.37 us -> 0.54 us  [gate_and_base(): pl.pallas_call(gate_kernel, out_shape=(jax.ShapeDtypeStruct((MB, W), F32)...]
    pallas_call x1, Pallas kernels: 2.05 us -> 0.31 us  [mix(): pl.pallas_call(mix_kernel, out_shape=jax.ShapeDtypeStruct((MP, MB, MSG),...]
  transfers between devices with their start and end apart: 4 -> 1, of which waited for: 4 -> 1; matrix products, arithmetic and copies ran while one was open for 2% -> 2% of each run, Pallas kernels for 2% -> 1%
where the time goes in v2:
time: 86.2 us; the launch traced here: 85.1 us
  blocking collectives  51 us (59%)
  starting transfers between devices  15.7 us (18%)
  Pallas kernels  8.62 us (10%)
  waiting for transfers between devices  4.45 us (5%)
  local copies, waits for them, and re-layouts  2.28 us (3%)
  other arithmetic  1.64 us (2%)
  between operations  1.44 us (2%)
    all_to_all x4, blocking collectives, exchange(): lax.all_to_all(x, axes, split_axis=0, concat_axis=0, tiled=True, axis_ind...  48.5 us
    all_to_all x1, starting transfers between devices, exchange(): lax.all_to_all(x, axes, split_axis=0, concat_axis=0, tiled=True, axis_ind...  15.7 us
    all_to_all x1, waiting for transfers between devices, exchange(): lax.all_to_all(x, axes, split_axis=0, concat_axis=0, tiled=True, axis_ind...  4.45 us
    pallas_call x1, Pallas kernels, attend(): pl.pallas_call(attend_kernel, out_shape=(jax.ShapeDtypeStruct((XC, ZROWS,...  4.37 us
    pallas_call x1, Pallas kernels, project(): pl.pallas_call(project_kernel, out_shape=(jax.ShapeDtypeStruct((NZ, MB, W...  2.56 us
    all_gather x1, blocking collectives, per_device(): arrived = lax.all_gather(arrived, 'core', axis=0)  2.5 us
    unnamed x24, local copies, waits for them, and re-layouts  1.93 us
  transfers between devices with their start and end apart: 1, of which 1 were waited for; matrix products, arithmetic and copies ran while one was open for 2% of the time, Pallas kernels for 1%

profile of v2, /device:TPU:6, one launch (start us, length us, event | category | flops | bytes accessed | tf_op | source)
XLA Modules:
  0.0 85.1 jit_solution(4660362493583914809)
XLA Ops:
  0.6 0.0 copy-start
  0.6 0.0 copy-start.1
  0.7 2.6 %project.1 = (bf16[16,8,384]{2,1,0:T(8,128)(2,1)}, bf16[128,256]{1,0:T(8,128)(2,1)}, bf16[128,256]{1,0:T(8,128)(2,1)}) custom-call(bf16[8,1024]{1,0:T(8,128)(2,1)} %cand.5, bf16[2,1024]{1,0:T(2,128)(2,1)} %act.1, bf16[1024,256]{1,0:T(8,128)(2,1)} %wq.1, bf16[1024,256]{1,0:T(8,128)(2,1)} %wk.1, bf16[1024,256]{1,0:T(8,128)(2,1)} %wv.1), custom_call_target="tpu_custom_call" | custom-call | tf_op jit(solution)/shard_map/gather/project/pallas_call | solution.py:92
  3.2 15.7 %all-to-all-start = ((bf16[16,8,384]{2,1,0:T(8,128)(2,1)}), bf16[16,8,384]{2,1,0:T(8,128)(2,1)S(1)}, u32[]{:S(2)}, u32[]{:S(2)}) async-start(bf16[16,8,384]{2,1,0:T(8,128)(2,1)} %get-tuple-element.17), calls=%async_computation | async-start | bytes 196608 | tf_op jit(solution)/shard_map/gather/all_to_all | solution.py:344
  18.9 0.0 copy-start.11
  18.9 0.0 copy-start.8
  18.9 0.0 copy-start.10
  19.0 0.6 copy-done.8
  19.6 0.6 fusion.4
  20.9 0.0 copy-start.7
  20.9 0.0 copy-done.11
  20.9 0.6 copy-done.7
  21.6 0.2 select_reduce_fusion
  21.7 0.2 compare_reduce_fusion
  22.0 0.1 select_reduce_fusion.1
  22.1 0.0 copy-start.4
  22.1 0.2 fusion
  22.3 0.0 copy-done.10
  22.3 0.1 dynamic_slice.3
  22.4 0.1 fusion.2
  22.4 0.1 add_bitcast_fusion
  22.5 0.1 copy.24
  22.6 0.1 copy.23
  22.7 0.1 copy.25
  22.8 0.0 copy-done
  22.8 0.0 copy-done.1
  22.8 0.0 copy-done.4
  22.8 0.5 gate.1
  23.3 0.0 copy-start.9
  23.3 0.1 pad_add_fusion.info
  23.4 0.6 copy-done.9
  24.0 0.1 compare_convert_fusion.maskrow
  24.1 4.4 %all-to-all-done = bf16[16,8,384]{2,1,0:T(8,128)(2,1)S(1)} async-done(((bf16[16,8,384]{2,1,0:T(8,128)(2,1)}), bf16[16,8,384]{2,1,0:T(8,128)(2,1)S(1)}, u32[]{:S(2)}, u32[]{:S(2)}) %all-to-all-start) | async-done | bytes 98336 | tf_op jit(solution)/shard_map/gather/all_to_all | solution.py:344
  28.6 9.9 %all_to_all.31 = bf16[4,128,384]{2,1,0:T(8,128)(2,1)S(1)} all-to-all(bf16[4,128,384]{2,1,0:T(8,128)(2,1)S(1)} %spread.1), channel_id=1, replica_groups=mesh['z'=16,'x'=4,'core'=2,'mp'=4] {'x'}, dimensions={0} | all-to-all | bytes 786432 | tf_op jit(solution)/shard_map/gather/all_to_all | solution.py:344
  38.5 0.0 copy-start.2
  38.5 0.0 copy-start.3
  38.5 0.0 copy-start.5
  38.5 0.0 copy-start.6
  38.5 2.5 %all-gather.arr = bf16[8,128,384]{2,1,0:T(8,128)(2,1)S(1)} all-gather(bf16[4,128,384]{2,1,0:T(8,128)(2,1)S(1)} %all_to_all.31), channel_id=2, replica_groups=mesh['z'=16,'x'=4,'core'=2,'mp'=4] {'core'}, dimensions={0}, use_global_device_ids=true | all-gather | bytes 1179648 | tf_op jit(solution)/shard_map/gather/all_gather | solution.py:408
  41.0 0.0 copy-done.2
  41.0 0.0 copy-done.3
  41.0 0.0 copy-done.5
  41.0 0.0 copy-done.6
  41.0 4.4 %attend.1 = (bf16[8,128,256]{2,1,0:T(8,128)(2,1)S(1)}, bf16[1024,256]{1,0:T(8,128)(2,1)}, bf16[1024,256]{1,0:T(8,128)(2,1)}) custom-call(s32[3,3]{1,0:T(4,128)S(1)} %pad_add_fusion.info, bf16[8,128]{1,0:T(8,128)(2,1)S(1)} %compare_convert_fusion.maskrow, bf16[8,128,384]{2,1,0:T(8,128)(2,1)S(1)} %all-gather.arr, bf16[128,256]{1,0:T(8,128)(2,1)S(1)} %copy-done.5, ...), custom_call_target="tpu_custom_call" | custom-call | tf_op jit(solution)/shard_map/attend/attend/pallas_call | solution.py:226
  45.4 12.8 %all_to_all.32.arr = bf16[8,128,256]{2,1,0:T(8,128)(2,1)S(1)} all-to-all(bf16[8,128,256]{2,1,0:T(8,128)(2,1)S(1)} %get-tuple-element.26), channel_id=1, replica_groups=mesh['z'=16,'x'=4,'core'=2,'mp'=4] {'x','core'}, dimensions={0} | all-to-all | bytes 1048576 | tf_op jit(solution)/shard_map/return/all_to_all | solution.py:344
  58.2 0.1 fold.1
  58.2 15.8 %all_to_all.33 = bf16[16,8,256]{2,1,0:T(8,128)(2,1)S(1)} all-to-all(bf16[16,8,256]{2,1,0:T(8,128)(2,1)S(1)} %bitcast.12), channel_id=1, replica_groups={{384,416,448,480,0,32,64,96,128,160,192,224,256,288,320,352},{385,417,4..., dimensions={0} | all-to-all | bytes 131072 | tf_op jit(solution)/shard_map/return/all_to_all | solution.py:344
  74.1 0.3 mix.1
  74.4 10.0 %all_to_all.34.arr = f32[4,8,640]{2,1,0:T(8,128)S(1)} all-to-all(f32[4,8,640]{2,1,0:T(8,128)S(1)} %mix.1), channel_id=1, replica_groups=mesh['z'=16,'x'=4,'core'=2,'mp'=4] {'mp'}, dimensions={0} | all-to-all | bytes 163840 | tf_op jit(solution)/shard_map/mix/all_to_all | solution.py:344
  84.3 0.8 finish.1
  (4 shorter events, 0.0 us)
Async XLA Ops:
  0.6 22.2 %copy-start = (bf16[256,1024]{1,0:T(8,128)(2,1)S(1)}, bf16[256,1024]{1,0:T(8,128)(2,1)}, u32[]{:S(2)}) copy-start(bf16[256,1024]{1,0:T(8,128)(2,1)} %wo.3) | copy-start | bytes 1572868
  0.6 22.1 %copy-start.1 = (bf16[1024,256]{1,0:T(8,128)(2,1)S(1)}, bf16[1024,256]{1,0:T(8,128)(2,1)}, u32[]{:S(2)}) copy-start(bf16[1024,256]{1,0:T(8,128)(2,1)} %wg.1) | copy-start | bytes 1572868
  3.2 25.3 %all-to-all-start = ((bf16[16,8,384]{2,1,0:T(8,128)(2,1)}), bf16[16,8,384]{2,1,0:T(8,128)(2,1)S(1)}, u32[]{:S(2)}, u32[]{:S(2)}) async-start(bf16[16,8,384]{2,1,0:T(8,128)(2,1)} %get-tuple-element.17), calls=%async_computation | async-start | bytes 196608 | tf_op jit(solution)/shard_map/gather/all_to_all | solution.py:344
  18.9 2.0 %copy-start.11 = (s32[4]{0:T(128)S(1)}, s32[4]{0:T(128)}, u32[]{:S(2)}) copy-start(s32[4]{0:T(128)} %param.24) | copy-start | bytes 52
  18.9 0.7 copy-start.8
  18.9 3.3 %copy-start.10 = (s32[256]{0:T(256)S(1)}, s32[256]{0:T(256)}, u32[]{:S(2)}) copy-start(s32[256]{0:T(256)} %param.25) | copy-start | bytes 3076
  20.9 0.7 copy-start.7
  22.1 0.7 copy-start.4
  23.3 0.7 copy-start.9
  38.5 2.5 %copy-start.2 = (bf16[1024,256]{1,0:T(8,128)(2,1)S(1)}, bf16[1024,256]{1,0:T(8,128)(2,1)}, u32[]{:S(2)}) copy-start(bf16[1024,256]{1,0:T(8,128)(2,1)} %keys.1) | copy-start | bytes 1572868
  38.5 2.5 %copy-start.3 = (bf16[1024,256]{1,0:T(8,128)(2,1)S(1)}, bf16[1024,256]{1,0:T(8,128)(2,1)}, u32[]{:S(2)}) copy-start(bf16[1024,256]{1,0:T(8,128)(2,1)} %vals.1) | copy-start | bytes 1572868
  38.5 2.5 %copy-start.5 = (bf16[128,256]{1,0:T(8,128)(2,1)S(1)}, bf16[128,256]{1,0:T(8,128)(2,1)}, u32[]{:S(2)}) copy-start(bf16[128,256]{1,0:T(8,128)(2,1)} %get-tuple-element.24.kx) | copy-start | bytes 196612
  38.5 2.5 %copy-start.6 = (bf16[128,256]{1,0:T(8,128)(2,1)S(1)}, bf16[128,256]{1,0:T(8,128)(2,1)}, u32[]{:S(2)}) copy-start(bf16[128,256]{1,0:T(8,128)(2,1)} %get-tuple-element.25.vx) | copy-start | bytes 196612

commit v3 on v2

v3 whole, which is shorter than its diff:
```python
import functools
import math

import jax
import jax.numpy as jnp
from jax import lax
from jax.experimental import pallas as pl
from jax.experimental.pallas import tpu as pltpu
from jax.sharding import Mesh
from jax.sharding import PartitionSpec as P

D = 1024
DH = 128
SEG = 512
NEW = 64
USERS = 4
NZ = 16
NX = 4
NC = 2
XC = NX * NC
ZX = NZ * NX
MP = 4
MB = 8
SEG_DEV = 2
W = D // MP
HEADS = W // DH
BATCHES = NZ * XC
QROWS = BATCHES * MB
HALF = ZX * MB
ZROWS = NZ * MB
FIRST_Z = 8
RETURN_Z = 8
TURN = (FIRST_Z - RETURN_Z) % NZ * MB
STORED = SEG_DEV * SEG
OWN = 16
ACT = 2
SCALE = 1.0 / math.sqrt(DH)
LOG2E = 1.4426950408889634
BF = jnp.bfloat16
F32 = jnp.float32
MIB = 1024 * 1024


def vspec():
    return pl.BlockSpec(memory_space=pltpu.VMEM)


def sspec():
    return pl.BlockSpec(memory_space=pltpu.SMEM)


def aspec():
    return pl.BlockSpec(memory_space=pl.ANY)


def params(mib):
    return pltpu.CompilerParams(vmem_limit_bytes=mib * MIB)


def cost(flops, nbytes):
    return pl.CostEstimate(flops=flops, bytes_accessed=nbytes, transcendentals=0)


def place():
    core = lax.axis_index("core")
    return core, lax.axis_index("z") * XC + lax.axis_index("x") * NC + core


def project_kernel(*refs):
    small, big, outs = refs[:5], refs[5:10], refs[10:14]
    scalars, vectors, weights = refs[14:18], refs[18:20], refs[20:25]
    rows, block, marks, sems = refs[25:]
    msg, own, info, mask = outs
    heavy = [pltpu.make_async_copy(x, y, sems.at[i]) for i, (x, y) in enumerate(zip(big, weights))]
    sources = small[:4] + (small[0], small[4])
    light = [
        pltpu.make_async_copy(x, y, sems.at[5 + i])
        for i, (x, y) in enumerate(zip(sources, scalars + vectors))
    ]
    for copy in heavy[:2] + light + heavy[2:]:
        copy.start()
    block[...] = jnp.zeros_like(block)
    marks[...] = jnp.zeros_like(marks)
    for copy in light:
        copy.wait()

    lists, counts, lengths, news = scalars
    core, device = place()
    ends = [lists[u, counts[u] - 1] for u in range(USERS)]
    for s in range(SEG_DEV):
        segment = device * SEG_DEV + s
        added = jnp.int32(0)
        user = jnp.int32(0)
        for u in range(USERS):
            hit = ends[u] == segment
            added = jnp.where(hit, news[u], added)
            user = jnp.where(hit, u, user)
        info[s, 0] = lengths[segment]
        info[s, 1] = added
        info[s, 2] = user

    act_user = device * ACT // NEW
    listed = vectors[0][...]
    listing = lax.broadcasted_iota(jnp.int32, listed.shape, 0).astype(F32)
    users = vectors[1][...]
    batch = users.astype(F32)
    for c in range(NC):
        near = device if c == 0 else device + 1 - 2 * core
        for s in range(SEG_DEV):
            hit = listed == near * SEG_DEV + s
            owner = jnp.sum(jnp.where(hit, listing, 0.0), axis=0, keepdims=True)
            owner = jnp.sum(owner, axis=1, keepdims=True)
            k = c * SEG_DEV + s
            marks[k : k + 1] = jnp.where(batch == owner, 1.0, 0.0)
    marks[4:5] = jnp.where(users == act_user, 1.0, 0.0)
    mask[...] = marks[...].astype(BF)

    c, q, a, k, v = weights
    heavy[0].wait()
    heavy[1].wait()
    query = jnp.dot(c[...], q[...], preferred_element_type=F32).astype(BF)
    heavy[2].wait()
    heavy[3].wait()
    key = jnp.dot(a[...], k[...], preferred_element_type=F32)
    heavy[4].wait()
    value = jnp.dot(a[...], v[...], preferred_element_type=F32)
    block[0:2] = key
    block[2:4] = value
    for h in range(HEADS):
        rows[h * 4 : h * 4 + 4] = block[0:4, h * DH : (h + 1) * DH]
    fresh = rows[...].astype(BF)
    for i in range(NZ):
        msg[i, :, 0:W] = query
        msg[i, :, W : W + DH] = fresh
    valid = jnp.clip(news[act_user] - device * ACT % NEW, 0, ACT)
    row = lax.broadcasted_iota(jnp.int32, (ACT, W), 0)
    block[2:4] = jnp.where(row < valid, value, 0.0)
    own[...] = block[...].astype(BF)


def project(lists, counts, lengths, news, users, cand, act, wq, wk, wv):
    weight = pltpu.VMEM((D, W), BF)
    return pl.pallas_call(
        project_kernel,
        out_shape=(
            jax.ShapeDtypeStruct((NZ, MB, W + DH), BF),
            jax.ShapeDtypeStruct((OWN, W), BF),
            jax.ShapeDtypeStruct((SEG_DEV, 3), jnp.int32),
            jax.ShapeDtypeStruct((8, BATCHES), BF),
        ),
        in_specs=[aspec()] * 10,
        out_specs=(vspec(), vspec(), sspec(), vspec()),
        scratch_shapes=[
            pltpu.SMEM(lists.shape, jnp.int32),
            pltpu.SMEM(counts.shape, jnp.int32),
            pltpu.SMEM(lengths.shape, jnp.int32),
            pltpu.SMEM(news.shape, jnp.int32),
            pltpu.VMEM(lists.shape, jnp.int32),
            pltpu.VMEM((1, BATCHES), jnp.int32),
            pltpu.VMEM((MB, D), BF),
            weight,
            pltpu.VMEM((ACT, D), BF),
            weight,
            weight,
            pltpu.VMEM((MB, DH), F32),
            pltpu.VMEM((OWN, W), F32),
            pltpu.VMEM((8, BATCHES), F32),
            pltpu.SemaphoreType.DMA((11,)),
        ],
        name="project",
    )(lists, counts, lengths, news, users.reshape(1, BATCHES), cand, wq, act, wk, wv)


def stage_kernel(info, own, keys, vals, out):
    out[0:STORED] = keys[...]
    rowpos = lax.broadcasted_iota(jnp.int32, (SEG, W), 0)
    for s in range(SEG_DEV):
        v = vals[s * SEG : (s + 1) * SEG].astype(F32)
        lo = STORED + s * SEG
        out[lo : lo + SEG] = jnp.where(rowpos < info[s, 0], v, 0.0).astype(BF)
    out[2 * STORED :] = own[...]


def stage(info, own, keys, vals):
    return pl.pallas_call(
        stage_kernel,
        out_shape=jax.ShapeDtypeStruct((2 * STORED + OWN, W), BF),
        in_specs=[sspec()] + [vspec()] * 3,
        out_specs=vspec(),
        compiler_params=params(16),
        cost_estimate=cost(1_000_000, 2_200_000),
        name="stage",
    )(info, own, keys, vals)


def spread_kernel(arr, out):
    rows = arr[...]
    for t in range(NX):
        out[t] = rows


def spread(arr):
    return pl.pallas_call(
        spread_kernel,
        out_shape=jax.ShapeDtypeStruct((NX, ZROWS, W + DH), BF),
        in_specs=[vspec()],
        out_specs=vspec(),
        compiler_params=params(8),
        name="spread",
    )(arr)


def append_kernel(info, arr, keys, vals, new_keys, new_vals):
    s = pl.program_id(0)
    length = info[s, 0]
    added = info[s, 1]
    user = info[s, 2]
    start = ((user * 4 + (NZ - FIRST_Z)) % NZ) * MB
    fresh = arr[:, pl.ds(pl.multiple_of(start, 4 * MB), 4 * MB), :].reshape(XC * 4 * MB, DH)
    shape = (SEG, XC * 4 * MB)
    pos = lax.broadcasted_iota(jnp.int32, shape, 0) - length
    j = lax.broadcasted_iota(jnp.int32, shape, 1)
    source = ((j // 32) % NX) * NC + j // 128
    step = ((j // 8) % 4) * 16 + source * 2 + j % 2
    kind = (j // 2) % 4
    rowpos = lax.broadcasted_iota(jnp.int32, (SEG, DH), 0)
    fill = (rowpos >= length) & (rowpos < length + added)
    for h in range(HEADS):
        cs = slice(h * DH, (h + 1) * DH)
        for i, (old, new) in enumerate(((keys, new_keys), (vals, new_vals))):
            hot = ((pos == step) & (kind == 2 * h + i)).astype(F32).astype(BF)
            placed = jnp.dot(hot, fresh, preferred_element_type=F32)
            new[:, cs] = jnp.where(fill, placed, old[:, cs].astype(F32)).astype(BF)


def append(info, arr, keys, vals):
    rows = SEG_DEV * SEG
    block = pl.BlockSpec((SEG, W), lambda s: (s, 0))
    return pl.pallas_call(
        append_kernel,
        grid=(SEG_DEV,),
        out_shape=(jax.ShapeDtypeStruct((rows, W), BF),) * 2,
        in_specs=[sspec(), pl.BlockSpec((XC, ZROWS, DH), lambda s: (0, 0, 0)), block, block],
        out_specs=(block, block),
        compiler_params=params(16),
        cost_estimate=cost(150_000_000, 2_500_000),
        name="append",
    )(info, arr, keys, vals)


def attend_kernel(maskrow, arr, mine, other, part, fresh, theirs, total, kx, vx, sem):
    copy = pltpu.make_async_copy(other, theirs, sem)
    copy.start()
    fresh[...] = arr[:, :, W:]
    shape = (HALF, BATCHES)
    row = lax.broadcasted_iota(jnp.int32, shape, 0)
    lane = lax.broadcasted_iota(jnp.int32, shape, 1)
    step = (row % ZROWS) // MB
    batch = ((step + FIRST_Z) % NZ) * XC + (row // ZROWS) * NC + lax.axis_index("core")
    hot = (lane == batch).astype(F32).astype(BF)
    use = lax.dot_general(
        hot, maskrow[...], (((1,), (1,)), ((), ())), preferred_element_type=F32
    )

    def weigh(logits):
        e = jnp.exp2(logits * (-SCALE * LOG2E))
        return (logits * SCALE) * pl.reciprocal(1.0 + e, approx=True)

    def score(a, b):
        return lax.dot_general(a, b, (((1,), (1,)), ((), ())), preferred_element_type=F32)

    def stored(c, src, h):
        cs = slice(h * DH, (h + 1) * DH)
        logits = score(q[:, cs], src[0:STORED, cs])
        parts = []
        for s in range(SEG_DEV):
            u = c * SEG_DEV + s
            seg = weigh(logits[:, s * SEG : (s + 1) * SEG]) * use[:, u : u + 1]
            parts.append(seg.astype(BF))
        wt = jnp.concatenate(parts, axis=1)
        return jnp.dot(wt, src[STORED : 2 * STORED, cs], preferred_element_type=F32)

    q = arr[:, :, 0:W].reshape(HALF, W)
    for h in range(HEADS):
        total[:, h * DH : (h + 1) * DH] = stored(0, mine, h)
    copy.wait()

    kx[...] = jnp.zeros_like(kx)
    vx[...] = jnp.zeros_like(vx)
    column = lax.broadcasted_iota(jnp.int32, (ACT, W), 1) // DH
    for c, src in enumerate((mine, theirs)):
        own = src[2 * STORED :].astype(F32)
        for h in range(HEADS):
            lo = (c * HEADS + h) * ACT
            kx[lo : lo + ACT] = jnp.where(column == h, own[0:ACT], 0.0)
            vx[lo : lo + ACT] = jnp.where(column == h, own[ACT : 2 * ACT], 0.0)
    wx = weigh(score(q, kx[...].astype(BF))) * use[:, 4:5]
    ox = jnp.dot(wx.astype(BF), vx[...].astype(BF), preferred_element_type=F32)
    for h in range(HEADS):
        cs = slice(h * DH, (h + 1) * DH)
        out = (total[:, cs] + stored(1, theirs, h) + ox[:, cs]).astype(BF)
        for x in range(NX):
            lo = x * ZROWS
            hi = lo + ZROWS
            part[x, TURN:, cs] = out[lo : hi - TURN]
            if TURN:
                part[x, 0:TURN, cs] = out[hi - TURN : hi]


def attend(maskrow, arr, mine, theirs):
    return pl.pallas_call(
        attend_kernel,
        out_shape=(
            jax.ShapeDtypeStruct((NX, ZROWS, W), BF),
            jax.ShapeDtypeStruct((NX, ZROWS, DH), BF),
        ),
        in_specs=[vspec()] * 3 + [aspec()],
        out_specs=(vspec(),) * 2,
        scratch_shapes=[
            pltpu.VMEM((2 * STORED + OWN, W), BF),
            pltpu.VMEM((HALF, W), F32),
            pltpu.VMEM((DH, W), F32),
            pltpu.VMEM((DH, W), F32),
            pltpu.SemaphoreType.DMA,
        ],
        compiler_params=params(32),
        name="attend",
    )(maskrow, arr, mine, theirs)


def fold_kernel(arr, out):
    out[...] = jnp.sum(arr[...].astype(F32), axis=0).astype(BF)


def fold(arr):
    return pl.pallas_call(
        fold_kernel,
        out_shape=jax.ShapeDtypeStruct((ZROWS, W), BF),
        in_specs=[vspec()],
        out_specs=vspec(),
        compiler_params=params(8),
        name="fold",
    )(arr)


def two_terms(x):
    hi = x.astype(BF)
    lo = (x - hi.astype(F32)).astype(BF)
    return hi, lo


def gate_kernel(cand, wg, wo, gate, base, own):
    first = pl.multiple_of(lax.axis_index("mp") * W, W)
    own[...] = cand[:, pl.ds(first, W)].astype(F32)
    v = jnp.dot(cand[...], wg[...], preferred_element_type=F32)
    g = v / (1.0 + jnp.exp(-v))
    gate[...] = g
    hi, lo = two_terms(g)
    base[...] = jnp.dot(hi, wo[...], preferred_element_type=F32) + jnp.dot(
        lo, wo[...], preferred_element_type=F32
    )


def gate_and_base(cand, wg, wo):
    return pl.pallas_call(
        gate_kernel,
        out_shape=(
            jax.ShapeDtypeStruct((MB, W), F32),
            jax.ShapeDtypeStruct((MB, D), F32),
            jax.ShapeDtypeStruct((MB, W), F32),
        ),
        in_specs=[vspec()] * 3,
        out_specs=(vspec(),) * 3,
        compiler_params=params(8),
        cost_estimate=cost(10_000_000_000, 40_000_000),
        name="gate",
    )(cand, wg, wo)


MSG = 2 * W + 128


def mix_kernel(arr, gate, base, wo, out):
    att = jnp.sum(arr[...].astype(F32).reshape(NZ, MB, W), axis=0)
    mean = jnp.sum(att, axis=1, keepdims=True) * (1.0 / W)
    d = att - mean
    sq = jnp.sum(d * d, axis=1, keepdims=True)
    hi, lo = two_terms(d * gate[...])
    a = jnp.dot(hi, wo[...], preferred_element_type=F32) + jnp.dot(
        lo, wo[...], preferred_element_type=F32
    )
    b = base[...]
    lane = lax.broadcasted_iota(jnp.int32, (MB, 128), 1)
    stats = jnp.where(lane == 0, mean, sq)
    for i in range(MP):
        out[i, :, 0:W] = a[:, i * W : (i + 1) * W]
        out[i, :, W : 2 * W] = b[:, i * W : (i + 1) * W]
        out[i, :, 2 * W : MSG] = stats


def mix(arr, gate, base, wo):
    return pl.pallas_call(
        mix_kernel,
        out_shape=jax.ShapeDtypeStruct((MP, MB, MSG), F32),
        in_specs=[vspec()] * 4,
        out_specs=vspec(),
        compiler_params=params(8),
        name="mix",
    )(arr, gate, base, wo)


def finish_kernel(arr, own, out):
    means = [arr[i, :, 2 * W : 2 * W + 1] for i in range(MP)]
    mean = sum(means) * (1.0 / MP)
    square = sum(arr[i, :, 2 * W + 1 : 2 * W + 2] for i in range(MP))
    square = square + W * sum((m - mean) * (m - mean) for m in means)
    scale = lax.rsqrt(square * (1.0 / D) + 1e-05)
    total = sum(
        arr[i, :, 0:W] + (means[i] - mean) * arr[i, :, W : 2 * W] for i in range(MP)
    )
    out[...] = (own[...] + total * scale).astype(BF)


def finish(arr, own):
    return pl.pallas_call(
        finish_kernel,
        out_shape=jax.ShapeDtypeStruct((MB, W), BF),
        in_specs=[vspec()] * 2,
        out_specs=vspec(),
        compiler_params=params(8),
        name="finish",
    )(arr, own)


def exchange(x, axes, first=None):
    groups = None if first is None else [[(i + first) % NZ for i in range(NZ)]]
    return lax.all_to_all(
        x, axes, split_axis=0, concat_axis=0, tiled=True, axis_index_groups=groups
    )


def per_device(
    candidates,
    actions,
    hist_keys,
    hist_values,
    w_query,
    w_gate,
    w_key,
    w_value,
    w_out,
    segment_list,
    segment_count,
    segment_length,
    new_count,
    batch_user,
):
    with jax.named_scope("gather"):
        message, own, info, mask = project(
            segment_list,
            segment_count,
            segment_length,
            new_count,
            batch_user,
            candidates,
            actions,
            w_query,
            w_key,
            w_value,
        )
        arrived = exchange(message, "z", FIRST_Z)
    with jax.named_scope("share"):
        mine = stage(info, own, hist_keys, hist_values)
        theirs = lax.ppermute(mine, "core", [(0, 1), (1, 0)])
        gate, base, residual = gate_and_base(candidates, w_gate, w_out)
        arrived, gate, base, residual = lax.optimization_barrier(
            (arrived, gate, base, residual)
        )
    with jax.named_scope("gather"):
        arrived = exchange(spread(arrived.reshape(ZROWS, W + DH)), "x")
    with jax.named_scope("attend"):
        part, fresh = attend(mask, arrived, mine, theirs)
    with jax.named_scope("return"):
        part = exchange(part, "x")
    with jax.named_scope("append"):
        fresh = lax.all_gather(fresh, "core", axis=0).reshape(XC, ZROWS, DH)
        new_keys, new_values = append(info, fresh, hist_keys, hist_values)
    with jax.named_scope("return"):
        part, new_keys, new_values = lax.optimization_barrier((part, new_keys, new_values))
        summed = exchange(fold(part), "z", RETURN_Z)
    with jax.named_scope("mix"):
        mixed = exchange(mix(summed, gate, base, w_out), "mp")
        ranked = finish(mixed, residual)
    return (ranked, new_keys, new_values)


def solution(mesh):
    names = ("z", "x", "core", "mp")
    inner = Mesh(mesh.devices.reshape(NZ, NX, NC, MP), names)
    hist = ("z", "x", "core")
    in_specs = (
        P(hist, None),
        P(hist, None),
        P(hist, "mp"),
        P(hist, "mp"),
        P(None, "mp"),
        P(None, "mp"),
        P(None, "mp"),
        P(None, "mp"),
        P("mp", None),
        P(),
        P(),
        P(),
        P(),
        P(),
    )
    out_specs = (P(hist, "mp"), P(hist, "mp"), P(hist, "mp"))
    return jax.shard_map(
        per_device, mesh=inner, in_specs=in_specs, out_specs=out_specs, check_vma=False
    )
```

time: 86.2 us -> 80.6 us (0.935)
  blocking collectives: 51 us -> 38.4 us
  starting transfers between devices: 15.7 us -> 26.2 us
  waiting for transfers between devices: 4.45 us -> 0.78 us
  Pallas kernels: 8.62 us -> 11.6 us
  other arithmetic: 1.64 us -> 0 us
  local copies, waits for them, and re-layouts: 2.28 us -> 1.36 us
    all_to_all x4 -> x3, blocking collectives: 48.5 us -> 36.3 us  [exchange(): lax.all_to_all(x, axes, split_axis=0, concat_axis=0, tiled=True, axis_ind...]
    all_to_all x1 -> x2, starting transfers between devices: 15.7 us -> 24.3 us  [exchange(): lax.all_to_all(x, axes, split_axis=0, concat_axis=0, tiled=True, axis_ind...]
    all_to_all x1 -> x2, waiting for transfers between devices: 4.45 us -> 0.77 us  [exchange(): lax.all_to_all(x, axes, split_axis=0, concat_axis=0, tiled=True, axis_ind...]
    pallas_call x1 -> x3, Pallas kernels: 4.37 us -> 7.28 us  [the longest x1 4.32 us: attend(): pl.pallas_call(attend_kernel, out_shape=(jax.ShapeDtypeStruct((NX, ZROWS,...]
    ppermute x0 -> x1, starting transfers between devices: none -> 1.92 us  [per_device(): theirs = lax.ppermute(mine, 'core', [(0, 1), (1, 0)])]
    reduce_sum x4 -> x0, other arithmetic: 1.11 us -> none  [the longest x1 0.63 us: per_device(): act_count = jnp.sum(jnp.where(user_ids == act_user, new_count, 0))]
    unnamed x24 -> x20, local copies, waits for them, and re-layouts: 1.93 us -> 1.36 us
  transfers between devices with their start and end apart: 1 -> 3, of which waited for: 1 -> 2; matrix products, arithmetic and copies ran while one was open for 2% -> 0% of each run, Pallas kernels for 1% -> 4%
where the time goes in v3:
time: 80.6 us; the launch traced here: 79.1 us
  blocking collectives  38.4 us (48%)
  starting transfers between devices  26.2 us (33%)
  Pallas kernels  11.6 us (14%)
  local copies, waits for them, and re-layouts  1.36 us (2%)
    all_to_all x3, blocking collectives, exchange(): lax.all_to_all(x, axes, split_axis=0, concat_axis=0, tiled=True, axis_ind...  36.3 us
    all_to_all x2, starting transfers between devices, exchange(): lax.all_to_all(x, axes, split_axis=0, concat_axis=0, tiled=True, axis_ind...  24.3 us
    pallas_call x1, Pallas kernels, attend(): pl.pallas_call(attend_kernel, out_shape=(jax.ShapeDtypeStruct((NX, ZROWS,...  4.32 us
    pallas_call x1, Pallas kernels, project(): pl.pallas_call(project_kernel, out_shape=(jax.ShapeDtypeStruct((NZ, MB, W...  2.62 us
    pallas_call x1, Pallas kernels, append(): pl.pallas_call(append_kernel, grid=(SEG_DEV,), out_shape=(jax.ShapeDtypeS...  2.27 us
    all_gather x1, blocking collectives, per_device(): fresh = lax.all_gather(fresh, 'core', axis=0).reshape(XC, ZROWS, DH)  2.11 us
    ppermute x1, starting transfers between devices, per_device(): theirs = lax.ppermute(mine, 'core', [(0, 1), (1, 0)])  1.92 us
  transfers between devices with their start and end apart: 3, of which 2 were waited for; matrix products, arithmetic and copies ran while one was open for 0% of the time, Pallas kernels for 4%

profile of v3, /device:TPU:6, one launch (start us, length us, event | category | flops | bytes accessed | tf_op | source)
XLA Modules:
  0.0 79.1 jit_solution(14914579560640291773)
XLA Ops:
  0.6 0.0 copy-start.1
  0.6 0.0 copy-start
  0.7 2.6 %project.1 = (bf16[16,8,384]{2,1,0:T(8,128)(2,1)}, bf16[16,256]{1,0:T(8,128)(2,1)}, s32[2,3]{1,0:T(2,128)}, bf16[8,128]{1,0:T(8,128)(2,1)}) custom-call(s32[4,128]{1,0:T(4,128)} %refs_0_.1, s32[4]{0:T(128)} %refs_1_.1, s32[256]{0:T(256)} %refs_2_.1, s32[4]{0:T(128)} %refs_3_.1, s32[1,128]{1,0:T(1,128)} %bitcast.7, bf16[8,1024]{1,0:T(8,128)(2,1)} %cand.1, ...), custom_call_target="tpu_custom_call" | custom-call | tf_op jit(solution)/shard_map/gather/project/pallas_call | solution.py:143
  3.3 18.9 %all-to-all-start = ((bf16[16,8,384]{2,1,0:T(8,128)(2,1)}), bf16[16,8,384]{2,1,0:T(8,128)(2,1)S(1)}, u32[]{:S(2)}, u32[]{:S(2)}) async-start(bf16[16,8,384]{2,1,0:T(8,128)(2,1)} %get-tuple-element.22), calls=%async_computation | async-start | bytes 196608 | tf_op jit(solution)/shard_map/gather/all_to_all | solution.py:437
  22.1 0.0 copy-done.1
  22.2 0.0 copy-done
  22.2 0.0 copy-start.5
  22.2 0.7 copy-done.5
  22.9 0.0 copy-start.6
  22.9 0.6 copy-done.6
  23.5 0.0 copy-start.2
  23.5 0.0 copy-start.4
  23.5 0.0 copy-start.9
  23.5 0.7 stage.1.mine
  24.2 1.9 %collective-permute-start = (bf16[2064,256]{1,0:T(8,128)(2,1)S(1)}, bf16[2064,256]{1,0:T(8,128)(2,1)S(1)}, u32[]{:S(2)}, u32[]{:S(2)}) collective-permute-start(bf16[2064,256]{1,0:T(8,128)(2,1)S(1)} %stage.1.mine), channel_id=1, source_target_pairs={{0,4},{4,0},{1,5},{5,1},{2,6},{6,2},{3,7},{7,3},{8,12},{12,8},{9,1... | collective-permute-start | bytes 3170312 | tf_op jit(solution)/shard_map/share/ppermute | solution.py:474
  26.1 0.0 copy-done.2
  26.1 0.0 copy-done.4
  26.1 0.0 copy-done.9
  26.2 0.5 gate.1
  26.7 0.0 copy-start.8
  26.7 0.6 all-to-all-done
  27.3 10.7 %all_to_all.31.arr = bf16[4,128,384]{2,1,0:T(8,128)(2,1)S(1)} all-to-all(bf16[4,128,384]{2,1,0:T(8,128)(2,1)S(1)} %spread.1), channel_id=1, replica_groups=mesh['z'=16,'x'=4,'core'=2,'mp'=4] {'x'}, dimensions={0} | all-to-all | bytes 786432 | tf_op jit(solution)/shard_map/gather/all_to_all | solution.py:437
  38.0 0.0 collective-permute-done.other
  38.0 0.0 copy-done.8
  38.0 0.0 copy-start.7
  38.0 4.3 %attend.1 = (bf16[4,128,256]{2,1,0:T(8,128)(2,1)}, bf16[4,128,128]{2,1,0:T(8,128)(2,1)S(1)}) custom-call(bf16[8,128]{1,0:T(8,128)(2,1)S(1)} %copy-done.8, bf16[4,128,384]{2,1,0:T(8,128)(2,1)S(1)} %all_to_all.31.arr, bf16[2064,256]{1,0:T(8,128)(2,1)S(1)} %stage.1.mine, bf16[2064,256]{1,0:T(8,128)(2,1)S(1)} %collective-permute-done.other), custom_call_target="tpu_custom_call" | custom-call | tf_op jit(solution)/shard_map/attend/attend/pallas_call | solution.py:311
  42.3 5.5 %all-to-all-start.2 = ((bf16[4,128,256]{2,1,0:T(8,128)(2,1)}), bf16[4,128,256]{2,1,0:T(8,128)(2,1)S(1)}, u32[]{:S(2)}, u32[]{:S(2)}) async-start(bf16[4,128,256]{2,1,0:T(8,128)(2,1)} %get-tuple-element.29), calls=%async_computation.2 | async-start | bytes 524288 | tf_op jit(solution)/shard_map/return/all_to_all | solution.py:437
  47.8 0.0 copy-start.3
  47.8 2.1 %all-gather.arr = bf16[8,128,128]{2,1,0:T(8,128)(2,1)S(1)} all-gather(bf16[4,128,128]{2,1,0:T(8,128)(2,1)S(1)} %get-tuple-element.30), channel_id=2, replica_groups=mesh['z'=16,'x'=4,'core'=2,'mp'=4] {'core'}, dimensions={0}, use_global_device_ids=true | all-gather | bytes 393216 | tf_op jit(solution)/shard_map/append/all_gather | solution.py:486
  49.9 0.0 copy-done.7
  49.9 2.3 %append.1 = (bf16[1024,256]{1,0:T(8,128)(2,1)}, bf16[1024,256]{1,0:T(8,128)(2,1)}) custom-call(s32[2,3]{1,0:T(2,128)S(1)} %copy-done.7, bf16[8,128,128]{2,1,0:T(8,128)(2,1)S(1)} %all-gather.arr, bf16[1024,256]{1,0:T(8,128)(2,1)S(1)} %copy-done, bf16[1024,256]{1,0:T(8,128)(2,1)S(1)} %copy-done.1), custom_call_target="tpu_custom_call" | custom-call | flops 150000000 | bytes 2500000 | tf_op jit(solution)/shard_map/append/append/pallas_call | solution.py:239
  52.2 0.2 all-to-all-done.2.arr
  52.4 15.6 %all_to_all.32 = bf16[16,8,256]{2,1,0:T(8,128)(2,1)S(1)} all-to-all(bf16[16,8,256]{2,1,0:T(8,128)(2,1)S(1)} %bitcast.5), channel_id=1, replica_groups={{256,288,320,352,384,416,448,480,0,32,64,96,128,160,192,224},{257,289,3..., dimensions={0} | all-to-all | bytes 131072 | tf_op jit(solution)/shard_map/return/all_to_all | solution.py:437
  68.1 0.0 copy-done.3
  68.1 0.3 mix.1
  68.4 10.0 %all_to_all.33.arr = f32[4,8,640]{2,1,0:T(8,128)S(1)} all-to-all(f32[4,8,640]{2,1,0:T(8,128)S(1)} %mix.1), channel_id=1, replica_groups=mesh['z'=16,'x'=4,'core'=2,'mp'=4] {'mp'}, dimensions={0} | all-to-all | bytes 163840 | tf_op jit(solution)/shard_map/mix/all_to_all | solution.py:437
  78.4 0.8 finish.1
  (2 shorter events, 0.1 us)
Async XLA Ops:
  0.6 21.5 %copy-start.1 = (bf16[1024,256]{1,0:T(8,128)(2,1)S(1)}, bf16[1024,256]{1,0:T(8,128)(2,1)}, u32[]{:S(2)}) copy-start(bf16[1024,256]{1,0:T(8,128)(2,1)} %vals.3) | copy-start | bytes 1572868
  0.6 21.5 %copy-start = (bf16[1024,256]{1,0:T(8,128)(2,1)S(1)}, bf16[1024,256]{1,0:T(8,128)(2,1)}, u32[]{:S(2)}) copy-start(bf16[1024,256]{1,0:T(8,128)(2,1)} %keys.3) | copy-start | bytes 1572868
  3.3 24.0 %all-to-all-start = ((bf16[16,8,384]{2,1,0:T(8,128)(2,1)}), bf16[16,8,384]{2,1,0:T(8,128)(2,1)S(1)}, u32[]{:S(2)}, u32[]{:S(2)}) async-start(bf16[16,8,384]{2,1,0:T(8,128)(2,1)} %get-tuple-element.22), calls=%async_computation | async-start | bytes 196608 | tf_op jit(solution)/shard_map/gather/all_to_all | solution.py:437
  22.2 0.7 copy-start.5
  22.9 0.6 copy-start.6
  23.5 2.6 %copy-start.2 = (bf16[256,1024]{1,0:T(8,128)(2,1)S(1)}, bf16[256,1024]{1,0:T(8,128)(2,1)}, u32[]{:S(2)}) copy-start(bf16[256,1024]{1,0:T(8,128)(2,1)} %wo.3) | copy-start | bytes 1572868
  23.5 2.6 %copy-start.4 = (bf16[8,1024]{1,0:T(8,128)(2,1)S(1)}, bf16[8,1024]{1,0:T(8,128)(2,1)}, u32[]{:S(2)}) copy-start(bf16[8,1024]{1,0:T(8,128)(2,1)} %cand.1) | copy-start | bytes 49156
  23.5 2.7 %copy-start.9 = (bf16[1024,256]{1,0:T(8,128)(2,1)S(1)}, bf16[1024,256]{1,0:T(8,128)(2,1)}, u32[]{:S(2)}) copy-start(bf16[1024,256]{1,0:T(8,128)(2,1)} %wg.1) | copy-start | bytes 1572868
  24.2 13.8 %collective-permute-start = (bf16[2064,256]{1,0:T(8,128)(2,1)S(1)}, bf16[2064,256]{1,0:T(8,128)(2,1)S(1)}, u32[]{:S(2)}, u32[]{:S(2)}) collective-permute-start(bf16[2064,256]{1,0:T(8,128)(2,1)S(1)} %stage.1.mine), channel_id=1, source_target_pairs={{0,4},{4,0},{1,5},{5,1},{2,6},{6,2},{3,7},{7,3},{8,12},{12,8},{9,1... | collective-permute-start | bytes 3170312 | tf_op jit(solution)/shard_map/share/ppermute | solution.py:474
  26.7 11.3 %copy-start.8 = (bf16[8,128]{1,0:T(8,128)(2,1)S(1)}, bf16[8,128]{1,0:T(8,128)(2,1)}, u32[]{:S(2)}) copy-start(bf16[8,128]{1,0:T(8,128)(2,1)} %get-tuple-element.21.maskrow) | copy-start | bytes 6148
  38.0 11.9 %copy-start.7 = (s32[2,3]{1,0:T(2,128)S(1)}, s32[2,3]{1,0:T(2,128)}, u32[]{:S(2)}) copy-start(s32[2,3]{1,0:T(2,128)} %get-tuple-element.27.info) | copy-start | bytes 76
  42.3 10.1 %all-to-all-start.2 = ((bf16[4,128,256]{2,1,0:T(8,128)(2,1)}), bf16[4,128,256]{2,1,0:T(8,128)(2,1)S(1)}, u32[]{:S(2)}, u32[]{:S(2)}) async-start(bf16[4,128,256]{2,1,0:T(8,128)(2,1)} %get-tuple-element.29), calls=%async_computation.2 | async-start | bytes 524288 | tf_op jit(solution)/shard_map/return/all_to_all | solution.py:437
  47.8 20.3 %copy-start.3 = (bf16[256,1024]{1,0:T(8,128)(2,1)S(1)}, bf16[256,1024]{1,0:T(8,128)(2,1)}, u32[]{:S(2)}) copy-start(bf16[256,1024]{1,0:T(8,128)(2,1)} %wo.3) | copy-start | bytes 1572868

commit v4 on v3

--- a/solution.py
+++ b/solution.py
@@ -29,8 +29,8 @@
 HALF = ZX * MB
 ZROWS = NZ * MB
 FIRST_Z = 8
-RETURN_Z = 8
-TURN = (FIRST_Z - RETURN_Z) % NZ * MB
+FIRST_X = 2
+FIRST_Y = 3
 STORED = SEG_DEV * SEG
 OWN = 16
 ACT = 2
@@ -134,8 +134,11 @@
         msg[i, :, W : W + DH] = fresh
     valid = jnp.clip(news[act_user] - device * ACT % NEW, 0, ACT)
     row = lax.broadcasted_iota(jnp.int32, (ACT, W), 0)
-    block[2:4] = jnp.where(row < valid, value, 0.0)
-    own[...] = block[...].astype(BF)
+    block[...] = jnp.zeros_like(block)
+    block[OWN - ACT : OWN] = key
+    own[0] = block[...].astype(BF)
+    block[OWN - ACT : OWN] = jnp.where(row < valid, value, 0.0)
+    own[1] = block[...].astype(BF)
 
 
 def project(lists, counts, lengths, news, users, cand, act, wq, wk, wv):
@@ -144,7 +147,7 @@
         project_kernel,
         out_shape=(
             jax.ShapeDtypeStruct((NZ, MB, W + DH), BF),
-            jax.ShapeDtypeStruct((OWN, W), BF),
+            jax.ShapeDtypeStruct((2, OWN, W), BF),
             jax.ShapeDtypeStruct((SEG_DEV, 3), jnp.int32),
             jax.ShapeDtypeStruct((8, BATCHES), BF),
         ),
@@ -172,19 +175,24 @@
 
 
 def stage_kernel(info, own, keys, vals, out):
-    out[0:STORED] = keys[...]
     rowpos = lax.broadcasted_iota(jnp.int32, (SEG, W), 0)
     for s in range(SEG_DEV):
-        v = vals[s * SEG : (s + 1) * SEG].astype(F32)
-        lo = STORED + s * SEG
+        lo = s * SEG
+        out[lo : lo + SEG] = keys[lo : lo + SEG]
+        v = vals[lo : lo + SEG].astype(F32)
+        lo += STORED
         out[lo : lo + SEG] = jnp.where(rowpos < info[s, 0], v, 0.0).astype(BF)
-    out[2 * STORED :] = own[...]
+    row = lax.broadcasted_iota(jnp.int32, (OWN, W), 0)
+    last = keys[SEG - OWN : SEG].astype(F32)
+    last = jnp.where(row >= OWN - ACT, own[0].astype(F32), last)
+    out[SEG - OWN : SEG] = last.astype(BF)
+    out[STORED + SEG - OWN : STORED + SEG] = own[1]
 
 
 def stage(info, own, keys, vals):
     return pl.pallas_call(
         stage_kernel,
-        out_shape=jax.ShapeDtypeStruct((2 * STORED + OWN, W), BF),
+        out_shape=jax.ShapeDtypeStruct((2 * STORED, W), BF),
         in_specs=[sspec()] + [vspec()] * 3,
         out_specs=vspec(),
         compiler_params=params(16),
@@ -220,7 +228,7 @@
     shape = (SEG, XC * 4 * MB)
     pos = lax.broadcasted_iota(jnp.int32, shape, 0) - length
     j = lax.broadcasted_iota(jnp.int32, shape, 1)
-    source = ((j // 32) % NX) * NC + j // 128
+    source = ((j // 32 + FIRST_X) % NX) * NC + j // 128
     step = ((j // 8) % 4) * 16 + source * 2 + j % 2
     kind = (j // 2) % 4
     rowpos = lax.broadcasted_iota(jnp.int32, (SEG, DH), 0)
@@ -248,7 +256,7 @@
     )(info, arr, keys, vals)
 
 
-def attend_kernel(maskrow, arr, mine, other, part, fresh, theirs, total, kx, vx, sem):
+def attend_kernel(maskrow, arr, mine, other, part, fresh, theirs, total, sem):
     copy = pltpu.make_async_copy(other, theirs, sem)
     copy.start()
     fresh[...] = arr[:, :, W:]
@@ -256,7 +264,8 @@
     row = lax.broadcasted_iota(jnp.int32, shape, 0)
     lane = lax.broadcasted_iota(jnp.int32, shape, 1)
     step = (row % ZROWS) // MB
-    batch = ((step + FIRST_Z) % NZ) * XC + (row // ZROWS) * NC + lax.axis_index("core")
+    column = (row // ZROWS + FIRST_X) % NX
+    batch = ((step + FIRST_Z) % NZ) * XC + column * NC + lax.axis_index("core")
     hot = (lane == batch).astype(F32).astype(BF)
     use = lax.dot_general(
         hot, maskrow[...], (((1,), (1,)), ((), ())), preferred_element_type=F32
@@ -268,15 +277,22 @@
 
     def score(a, b):
         return lax.dot_general(a, b, (((1,), (1,)), ((), ())), preferred_element_type=F32)
+
+    lane = lax.broadcasted_iota(jnp.int32, (HALF, DH), 1)
+    marks = []
+    for u in range(NC * SEG_DEV):
+        seg = jnp.broadcast_to(use[:, u : u + 1], (HALF, DH))
+        marks.append((seg, jnp.where(lane >= DH - ACT, use[:, 4:5], seg)))
 
     def stored(c, src, h):
         cs = slice(h * DH, (h + 1) * DH)
         logits = score(q[:, cs], src[0:STORED, cs])
         parts = []
-        for s in range(SEG_DEV):
-            u = c * SEG_DEV + s
-            seg = weigh(logits[:, s * SEG : (s + 1) * SEG]) * use[:, u : u + 1]
-            parts.append(seg.astype(BF))
+        for i in range(STORED // DH):
+            s = i * DH // SEG
+            last = s == 0 and (i + 1) * DH == SEG
+            mark = marks[c * SEG_DEV + s][1 if last else 0]
+            parts.append((weigh(logits[:, i * DH : (i + 1) * DH]) * mark).astype(BF))
         wt = jnp.concatenate(parts, axis=1)
         return jnp.dot(wt, src[STORED : 2 * STORED, cs], preferred_element_type=F32)
 
@@ -284,27 +300,11 @@
     for h in range(HEADS):
         total[:, h * DH : (h + 1) * DH] = stored(0, mine, h)
     copy.wait()
-
-    kx[...] = jnp.zeros_like(kx)
-    vx[...] = jnp.zeros_like(vx)
-    column = lax.broadcasted_iota(jnp.int32, (ACT, W), 1) // DH
-    for c, src in enumerate((mine, theirs)):
-        own = src[2 * STORED :].astype(F32)
-        for h in range(HEADS):
-            lo = (c * HEADS + h) * ACT
-            kx[lo : lo + ACT] = jnp.where(column == h, own[0:ACT], 0.0)
-            vx[lo : lo + ACT] = jnp.where(column == h, own[ACT : 2 * ACT], 0.0)
-    wx = weigh(score(q, kx[...].astype(BF))) * use[:, 4:5]
-    ox = jnp.dot(wx.astype(BF), vx[...].astype(BF), preferred_element_type=F32)
     for h in range(HEADS):
         cs = slice(h * DH, (h + 1) * DH)
-        out = (total[:, cs] + stored(1, theirs, h) + ox[:, cs]).astype(BF)
+        out = (total[:, cs] + stored(1, theirs, h)).astype(BF)
         for x in range(NX):
-            lo = x * ZROWS
-            hi = lo + ZROWS
-            part[x, TURN:, cs] = out[lo : hi - TURN]
-            if TURN:
-                part[x, 0:TURN, cs] = out[hi - TURN : hi]
+            part[x, :, cs] = out[x * ZROWS : (x + 1) * ZROWS]
 
 
 def attend(maskrow, arr, mine, theirs):
@@ -317,10 +317,8 @@
         in_specs=[vspec()] * 3 + [aspec()],
         out_specs=(vspec(),) * 2,
         scratch_shapes=[
-            pltpu.VMEM((2 * STORED + OWN, W), BF),
+            pltpu.VMEM((2 * STORED, W), BF),
             pltpu.VMEM((HALF, W), F32),
-            pltpu.VMEM((DH, W), F32),
-            pltpu.VMEM((DH, W), F32),
             pltpu.SemaphoreType.DMA,
         ],
         compiler_params=params(32),
@@ -393,8 +391,9 @@
     lane = lax.broadcasted_iota(jnp.int32, (MB, 128), 1)
     stats = jnp.where(lane == 0, mean, sq)
     for i in range(MP):
-        out[i, :, 0:W] = a[:, i * W : (i + 1) * W]
-        out[i, :, W : 2 * W] = b[:, i * W : (i + 1) * W]
+        cs = slice((i + FIRST_Y) % MP * W, ((i + FIRST_Y) % MP + 1) * W)
+        out[i, :, 0:W] = a[:, cs]
+        out[i, :, W : 2 * W] = b[:, cs]
         out[i, :, 2 * W : MSG] = stats
 
 
@@ -432,10 +431,10 @@
     )(arr, own)
 
 
-def exchange(x, axes, first=None):
-    groups = None if first is None else [[(i + first) % NZ for i in range(NZ)]]
+def exchange(x, axis, size, first):
+    groups = [[(i + first) % size for i in range(size)]]
     return lax.all_to_all(
-        x, axes, split_axis=0, concat_axis=0, tiled=True, axis_index_groups=groups
+        x, axis, split_axis=0, concat_axis=0, tiled=True, axis_index_groups=groups
     )
 
 
@@ -468,7 +467,7 @@
             w_key,
             w_value,
         )
-        arrived = exchange(message, "z", FIRST_Z)
+        arrived = exchange(message, "z", NZ, FIRST_Z)
     with jax.named_scope("share"):
         mine = stage(info, own, hist_keys, hist_values)
         theirs = lax.ppermute(mine, "core", [(0, 1), (1, 0)])
@@ -477,19 +476,19 @@
             (arrived, gate, base, residual)
         )
     with jax.named_scope("gather"):
-        arrived = exchange(spread(arrived.reshape(ZROWS, W + DH)), "x")
+        arrived = exchange(spread(arrived.reshape(ZROWS, W + DH)), "x", NX, FIRST_X)
     with jax.named_scope("attend"):
         part, fresh = attend(mask, arrived, mine, theirs)
     with jax.named_scope("return"):
-        part = exchange(part, "x")
+        part = exchange(part, "x", NX, FIRST_X)
     with jax.named_scope("append"):
         fresh = lax.all_gather(fresh, "core", axis=0).reshape(XC, ZROWS, DH)
         new_keys, new_values = append(info, fresh, hist_keys, hist_values)
     with jax.named_scope("return"):
         part, new_keys, new_values = lax.optimization_barrier((part, new_keys, new_values))
-        summed = exchange(fold(part), "z", RETURN_Z)
+        summed = exchange(fold(part), "z", NZ, FIRST_Z)
     with jax.named_scope("mix"):
-        mixed = exchange(mix(summed, gate, base, w_out), "mp")
+        mixed = exchange(mix(summed, gate, base, w_out), "mp", MP, FIRST_Y)
         ranked = finish(mixed, residual)
     return (ranked, new_keys, new_values)
 

time: 80.6 us -> 78.1 us (0.969)
  waiting for transfers between devices: 0.78 us -> 2.83 us
  blocking collectives: 38.4 us -> 36.5 us
  starting transfers between devices: 26.2 us -> 25.3 us
    all_to_all x2, waiting for transfers between devices: 0.77 us -> 2.83 us  [exchange(): lax.all_to_all(x, axis, split_axis=0, concat_axis=0, tiled=True, axis_ind...]
    all_to_all x3, blocking collectives: 36.3 us -> 34.5 us  [exchange(): lax.all_to_all(x, axis, split_axis=0, concat_axis=0, tiled=True, axis_ind...]
    all_to_all x2, starting transfers between devices: 24.3 us -> 23.4 us  [exchange(): lax.all_to_all(x, axis, split_axis=0, concat_axis=0, tiled=True, axis_ind...]
  transfers between devices with their start and end apart: 3 -> 3, of which waited for: 2 -> 2; matrix products, arithmetic and copies ran while one was open for 0% -> 0% of each run, Pallas kernels for 4% -> 5%
where the time goes in v4:
time: 78.1 us; the launch traced here: 77.1 us
  blocking collectives  36.5 us (47%)
  starting transfers between devices  25.3 us (32%)
  Pallas kernels  11.1 us (14%)
  waiting for transfers between devices  2.83 us (4%)
    all_to_all x3, blocking collectives, exchange(): lax.all_to_all(x, axis, split_axis=0, concat_axis=0, tiled=True, axis_ind...  34.5 us
    all_to_all x2, starting transfers between devices, exchange(): lax.all_to_all(x, axis, split_axis=0, concat_axis=0, tiled=True, axis_ind...  23.4 us
    pallas_call x1, Pallas kernels, attend(): pl.pallas_call(attend_kernel, out_shape=(jax.ShapeDtypeStruct((NX, ZROWS,...  3.9 us
    all_to_all x2, waiting for transfers between devices, exchange(): lax.all_to_all(x, axis, split_axis=0, concat_axis=0, tiled=True, axis_ind...  2.83 us
    pallas_call x1, Pallas kernels, project(): pl.pallas_call(project_kernel, out_shape=(jax.ShapeDtypeStruct((NZ, MB, W...  2.62 us
    pallas_call x1, Pallas kernels, append(): pl.pallas_call(append_kernel, grid=(SEG_DEV,), out_shape=(jax.ShapeDtypeS...  2.27 us
    all_gather x1, blocking collectives, per_device(): fresh = lax.all_gather(fresh, 'core', axis=0).reshape(XC, ZROWS, DH)  1.98 us
    ppermute x1, starting transfers between devices, per_device(): theirs = lax.ppermute(mine, 'core', [(0, 1), (1, 0)])  1.92 us
  transfers between devices with their start and end apart: 3, of which 2 were waited for; matrix products, arithmetic and copies ran while one was open for 0% of the time, Pallas kernels for 5%

profile of v4, /device:TPU:6, one launch (start us, length us, event | category | flops | bytes accessed | tf_op | source)
XLA Modules:
  0.0 77.1 jit_solution(12613177798033063631)
XLA Ops:
  0.6 0.0 copy-start
  0.6 0.0 copy-start.1
  0.7 2.6 %project.1 = (bf16[16,8,384]{2,1,0:T(8,128)(2,1)}, bf16[2,16,256]{2,1,0:T(8,128)(2,1)}, s32[2,3]{1,0:T(2,128)}, bf16[8,128]{1,0:T(8,128)(2,1)}) custom-call(s32[4,128]{1,0:T(4,128)} %refs_0_.1, s32[4]{0:T(128)} %refs_1_.1, s32[256]{0:T(256)} %refs_2_.1, s32[4]{0:T(128)} %refs_3_.1, s32[1,128]{1,0:T(1,128)} %bitcast.7, bf16[8,1024]{1,0:T(8,128)(2,1)} %cand.1, ...), custom_call_target="tpu_custom_call" | custom-call | tf_op jit(solution)/shard_map/gather/project/pallas_call | solution.py:146
  3.3 0.0 copy-start.5
  3.3 18.9 %all-to-all-start = ((bf16[16,8,384]{2,1,0:T(8,128)(2,1)}), bf16[16,8,384]{2,1,0:T(8,128)(2,1)S(1)}, u32[]{:S(2)}, u32[]{:S(2)}) async-start(bf16[16,8,384]{2,1,0:T(8,128)(2,1)} %get-tuple-element.22), calls=%async_computation | async-start | bytes 196608 | tf_op jit(solution)/shard_map/gather/all_to_all | solution.py:436
  22.2 0.0 copy-start.6
  22.2 0.0 copy-done
  22.2 0.0 copy-done.1
  22.2 0.0 copy-done.5
  22.2 0.6 copy-done.6
  22.8 0.0 copy-start.2
  22.8 0.0 copy-start.4
  22.8 0.0 copy-start.8
  22.8 0.7 stage.1.mine
  23.5 1.9 %collective-permute-start = (bf16[2048,256]{1,0:T(8,128)(2,1)S(1)}, bf16[2048,256]{1,0:T(8,128)(2,1)S(1)}, u32[]{:S(2)}, u32[]{:S(2)}) collective-permute-start(bf16[2048,256]{1,0:T(8,128)(2,1)S(1)} %stage.1.mine), channel_id=1, source_target_pairs={{0,4},{4,0},{1,5},{5,1},{2,6},{6,2},{3,7},{7,3},{8,12},{12,8},{9,1... | collective-permute-start | bytes 3145736 | tf_op jit(solution)/shard_map/share/ppermute | solution.py:473
  25.4 0.0 copy-done.2
  25.5 0.0 copy-done.4
  25.5 0.0 copy-done.8
  25.5 0.5 gate.1
  26.0 1.3 %all-to-all-done = bf16[16,8,384]{2,1,0:T(8,128)(2,1)S(1)} async-done(((bf16[16,8,384]{2,1,0:T(8,128)(2,1)}), bf16[16,8,384]{2,1,0:T(8,128)(2,1)S(1)}, u32[]{:S(2)}, u32[]{:S(2)}) %all-to-all-start) | async-done | bytes 98336 | tf_op jit(solution)/shard_map/gather/all_to_all | solution.py:436
  27.3 0.0 copy-start.7
  27.3 9.9 %all_to_all.31.arr = bf16[4,128,384]{2,1,0:T(8,128)(2,1)S(1)} all-to-all(bf16[4,128,384]{2,1,0:T(8,128)(2,1)S(1)} %spread.1), channel_id=1, replica_groups={{16,24,0,8},{17,25,1,9},{18,26,2,10},{19,27,3,11},{20,28,4,12},{21,29,5..., dimensions={0} | all-to-all | bytes 786432 | tf_op jit(solution)/shard_map/gather/all_to_all | solution.py:436
  37.2 0.0 collective-permute-done.other
  37.2 0.0 copy-done.7
  37.3 3.9 %attend.1 = (bf16[4,128,256]{2,1,0:T(8,128)(2,1)}, bf16[4,128,128]{2,1,0:T(8,128)(2,1)S(1)}) custom-call(bf16[8,128]{1,0:T(8,128)(2,1)S(1)} %copy-done.7, bf16[4,128,384]{2,1,0:T(8,128)(2,1)S(1)} %all_to_all.31.arr, bf16[2048,256]{1,0:T(8,128)(2,1)S(1)} %stage.1.mine, bf16[2048,256]{1,0:T(8,128)(2,1)S(1)} %collective-permute-done.other), custom_call_target="tpu_custom_call" | custom-call | tf_op jit(solution)/shard_map/attend/attend/pallas_call | solution.py:311
  41.2 4.5 %all-to-all-start.2 = ((bf16[4,128,256]{2,1,0:T(8,128)(2,1)}), bf16[4,128,256]{2,1,0:T(8,128)(2,1)S(1)}, u32[]{:S(2)}, u32[]{:S(2)}) async-start(bf16[4,128,256]{2,1,0:T(8,128)(2,1)} %get-tuple-element.29), calls=%async_computation.2 | async-start | bytes 524288 | tf_op jit(solution)/shard_map/return/all_to_all | solution.py:436
  45.6 2.0 %all-gather.arr = bf16[8,128,128]{2,1,0:T(8,128)(2,1)S(1)} all-gather(bf16[4,128,128]{2,1,0:T(8,128)(2,1)S(1)} %get-tuple-element.30), channel_id=2, replica_groups=mesh['z'=16,'x'=4,'core'=2,'mp'=4] {'core'}, dimensions={0}, use_global_device_ids=true | all-gather | bytes 393216 | tf_op jit(solution)/shard_map/append/all_gather | solution.py:485
  47.6 0.0 copy-start.3
  47.6 2.3 %append.1 = (bf16[1024,256]{1,0:T(8,128)(2,1)}, bf16[1024,256]{1,0:T(8,128)(2,1)}) custom-call(s32[2,3]{1,0:T(2,128)S(1)} %copy-done.6, bf16[8,128,128]{2,1,0:T(8,128)(2,1)S(1)} %all-gather.arr, bf16[1024,256]{1,0:T(8,128)(2,1)S(1)} %copy-done, bf16[1024,256]{1,0:T(8,128)(2,1)S(1)} %copy-done.1), custom_call_target="tpu_custom_call" | custom-call | flops 150000000 | bytes 2500000 | tf_op jit(solution)/shard_map/append/append/pallas_call | solution.py:247
  49.9 1.6 %all-to-all-done.2.arr = bf16[4,128,256]{2,1,0:T(8,128)(2,1)S(1)} async-done(((bf16[4,128,256]{2,1,0:T(8,128)(2,1)}), bf16[4,128,256]{2,1,0:T(8,128)(2,1)S(1)}, u32[]{:S(2)}, u32[]{:S(2)}) %all-to-all-start.2) | async-done | bytes 262176 | tf_op jit(solution)/shard_map/return/all_to_all | solution.py:436
  51.5 15.5 %all_to_all.32 = bf16[16,8,256]{2,1,0:T(8,128)(2,1)S(1)} all-to-all(bf16[16,8,256]{2,1,0:T(8,128)(2,1)S(1)} %bitcast.5), channel_id=1, replica_groups={{256,288,320,352,384,416,448,480,0,32,64,96,128,160,192,224},{257,289,3..., dimensions={0} | all-to-all | bytes 131072 | tf_op jit(solution)/shard_map/return/all_to_all | solution.py:436
  67.0 0.0 copy-done.3
  67.1 0.3 mix.1
  67.4 9.0 %all_to_all.33.arr = f32[4,8,640]{2,1,0:T(8,128)S(1)} all-to-all(f32[4,8,640]{2,1,0:T(8,128)S(1)} %mix.1), channel_id=1, replica_groups={{3,0,1,2},{7,4,5,6},{11,8,9,10},{15,12,13,14},{19,16,17,18},{23,20,21,2..., dimensions={0} | all-to-all | bytes 163840 | tf_op jit(solution)/shard_map/mix/all_to_all | solution.py:436
  76.4 0.8 finish.1
  (2 shorter events, 0.1 us)
Async XLA Ops:
  0.6 21.5 %copy-start = (bf16[1024,256]{1,0:T(8,128)(2,1)S(1)}, bf16[1024,256]{1,0:T(8,128)(2,1)}, u32[]{:S(2)}) copy-start(bf16[1024,256]{1,0:T(8,128)(2,1)} %keys.3) | copy-start | bytes 1572868
  0.6 21.5 %copy-start.1 = (bf16[1024,256]{1,0:T(8,128)(2,1)S(1)}, bf16[1024,256]{1,0:T(8,128)(2,1)}, u32[]{:S(2)}) copy-start(bf16[1024,256]{1,0:T(8,128)(2,1)} %vals.3) | copy-start | bytes 1572868
  3.3 18.9 %copy-start.5 = (bf16[2,16,256]{2,1,0:T(8,128)(2,1)S(1)}, bf16[2,16,256]{2,1,0:T(8,128)(2,1)}, u32[]{:S(2)}) copy-start(bf16[2,16,256]{2,1,0:T(8,128)(2,1)} %get-tuple-element.28.own) | copy-start | bytes 49156
  3.3 24.0 %all-to-all-start = ((bf16[16,8,384]{2,1,0:T(8,128)(2,1)}), bf16[16,8,384]{2,1,0:T(8,128)(2,1)S(1)}, u32[]{:S(2)}, u32[]{:S(2)}) async-start(bf16[16,8,384]{2,1,0:T(8,128)(2,1)} %get-tuple-element.22), calls=%async_computation | async-start | bytes 196608 | tf_op jit(solution)/shard_map/gather/all_to_all | solution.py:436
  22.2 0.7 copy-start.6
  22.8 2.6 %copy-start.2 = (bf16[256,1024]{1,0:T(8,128)(2,1)S(1)}, bf16[256,1024]{1,0:T(8,128)(2,1)}, u32[]{:S(2)}) copy-start(bf16[256,1024]{1,0:T(8,128)(2,1)} %wo.3) | copy-start | bytes 1572868
  22.8 2.6 %copy-start.4 = (bf16[8,1024]{1,0:T(8,128)(2,1)S(1)}, bf16[8,1024]{1,0:T(8,128)(2,1)}, u32[]{:S(2)}) copy-start(bf16[8,1024]{1,0:T(8,128)(2,1)} %cand.1) | copy-start | bytes 49156
  22.8 2.6 %copy-start.8 = (bf16[1024,256]{1,0:T(8,128)(2,1)S(1)}, bf16[1024,256]{1,0:T(8,128)(2,1)}, u32[]{:S(2)}) copy-start(bf16[1024,256]{1,0:T(8,128)(2,1)} %wg.1) | copy-start | bytes 1572868
  23.5 13.7 %collective-permute-start = (bf16[2048,256]{1,0:T(8,128)(2,1)S(1)}, bf16[2048,256]{1,0:T(8,128)(2,1)S(1)}, u32[]{:S(2)}, u32[]{:S(2)}) collective-permute-start(bf16[2048,256]{1,0:T(8,128)(2,1)S(1)} %stage.1.mine), channel_id=1, source_target_pairs={{0,4},{4,0},{1,5},{5,1},{2,6},{6,2},{3,7},{7,3},{8,12},{12,8},{9,1... | collective-permute-start | bytes 3145736 | tf_op jit(solution)/shard_map/share/ppermute | solution.py:473
  27.3 9.9 %copy-start.7 = (bf16[8,128]{1,0:T(8,128)(2,1)S(1)}, bf16[8,128]{1,0:T(8,128)(2,1)}, u32[]{:S(2)}) copy-start(bf16[8,128]{1,0:T(8,128)(2,1)} %get-tuple-element.21.maskrow) | copy-start | bytes 6148
  41.2 10.3 %all-to-all-start.2 = ((bf16[4,128,256]{2,1,0:T(8,128)(2,1)}), bf16[4,128,256]{2,1,0:T(8,128)(2,1)S(1)}, u32[]{:S(2)}, u32[]{:S(2)}) async-start(bf16[4,128,256]{2,1,0:T(8,128)(2,1)} %get-tuple-element.29), calls=%async_computation.2 | async-start | bytes 524288 | tf_op jit(solution)/shard_map/return/all_to_all | solution.py:436
  47.6 19.4 %copy-start.3 = (bf16[256,1024]{1,0:T(8,128)(2,1)S(1)}, bf16[256,1024]{1,0:T(8,128)(2,1)}, u32[]{:S(2)}) copy-start(bf16[256,1024]{1,0:T(8,128)(2,1)} %wo.3) | copy-start | bytes 1572868

commit v5 on v4

--- a/solution.py
+++ b/solution.py
@@ -33,6 +33,8 @@
 FIRST_Y = 3
 STORED = SEG_DEV * SEG
 OWN = 16
+PATCH = NEW + 16
+HEAD = SEG // 4
 ACT = 2
 SCALE = 1.0 / math.sqrt(DH)
 LOG2E = 1.4426950408889634
@@ -218,38 +220,62 @@
     )(arr)
 
 
-def append_kernel(info, arr, keys, vals, new_keys, new_vals):
-    s = pl.program_id(0)
-    length = info[s, 0]
-    added = info[s, 1]
-    user = info[s, 2]
-    start = ((user * 4 + (NZ - FIRST_Z)) % NZ) * MB
-    fresh = arr[:, pl.ds(pl.multiple_of(start, 4 * MB), 4 * MB), :].reshape(XC * 4 * MB, DH)
-    shape = (SEG, XC * 4 * MB)
-    pos = lax.broadcasted_iota(jnp.int32, shape, 0) - length
+def append_kernel(info, arr, keys, vals, new_keys, new_vals, patch, sems):
+    pairs = ((keys, new_keys), (vals, new_vals))
+    copies = []
+    for s in range(SEG_DEV):
+        rows = pl.ds(s * SEG, HEAD)
+        for i, (old, new) in enumerate(pairs):
+            copies.append(
+                pltpu.make_async_copy(old.at[rows], new.at[rows], sems.at[s * 2 + i])
+            )
+            copies[-1].start()
+
+    shape = (PATCH, XC * 4 * MB)
     j = lax.broadcasted_iota(jnp.int32, shape, 1)
     source = ((j // 32 + FIRST_X) % NX) * NC + j // 128
     step = ((j // 8) % 4) * 16 + source * 2 + j % 2
     kind = (j // 2) % 4
-    rowpos = lax.broadcasted_iota(jnp.int32, (SEG, DH), 0)
-    fill = (rowpos >= length) & (rowpos < length + added)
-    for h in range(HEADS):
-        cs = slice(h * DH, (h + 1) * DH)
-        for i, (old, new) in enumerate(((keys, new_keys), (vals, new_vals))):
-            hot = ((pos == step) & (kind == 2 * h + i)).astype(F32).astype(BF)
-            placed = jnp.dot(hot, fresh, preferred_element_type=F32)
-            new[:, cs] = jnp.where(fill, placed, old[:, cs].astype(F32)).astype(BF)
+    for s in range(SEG_DEV):
+        length = info[s, 0]
+        begin = jnp.clip((length // 16) * 16, HEAD, SEG - PATCH)
+        rows = pl.ds(pl.multiple_of(s * SEG + begin, 16), PATCH)
+        inner = pl.ds(pl.multiple_of(begin - HEAD, 16), PATCH)
+        tail = pl.ds(s * SEG + HEAD, SEG - HEAD)
+        start = ((info[s, 2] * 4 + (NZ - FIRST_Z)) % NZ) * MB
+        fresh = arr[:, pl.ds(pl.multiple_of(start, 4 * MB), 4 * MB), :]
+        fresh = fresh.reshape(XC * 4 * MB, DH)
+        match = lax.broadcasted_iota(jnp.int32, shape, 0) + (begin - length) == step
+        rowpos = lax.broadcasted_iota(jnp.int32, (PATCH, DH), 0) + (begin - length)
+        fill = (rowpos >= 0) & (rowpos < info[s, 1])
+        for i, (old, new) in enumerate(pairs):
+            slot = s * 2 + i
+            patch[slot] = old[tail]
+            for h in range(HEADS):
+                cs = slice(h * DH, (h + 1) * DH)
+                hot = (match & (kind == 2 * h + i)).astype(F32).astype(BF)
+                placed = jnp.dot(hot, fresh, preferred_element_type=F32)
+                kept = old[rows, cs].astype(F32)
+                patch[slot, inner, cs] = jnp.where(fill, placed, kept).astype(BF)
+            copies.append(
+                pltpu.make_async_copy(patch.at[slot], new.at[tail], sems.at[4 + slot])
+            )
+            copies[-1].start()
+    for copy in copies:
+        copy.wait()
 
 
 def append(info, arr, keys, vals):
-    rows = SEG_DEV * SEG
-    block = pl.BlockSpec((SEG, W), lambda s: (s, 0))
+    stored = jax.ShapeDtypeStruct((STORED, W), BF)
     return pl.pallas_call(
         append_kernel,
-        grid=(SEG_DEV,),
-        out_shape=(jax.ShapeDtypeStruct((rows, W), BF),) * 2,
-        in_specs=[sspec(), pl.BlockSpec((XC, ZROWS, DH), lambda s: (0, 0, 0)), block, block],
-        out_specs=(block, block),
+        out_shape=(stored,) * 2,
+        in_specs=[sspec()] + [vspec()] * 3,
+        out_specs=(aspec(),) * 2,
+        scratch_shapes=[
+            pltpu.VMEM((SEG_DEV * 2, SEG - HEAD, W), BF),
+            pltpu.SemaphoreType.DMA((SEG_DEV * 4,)),
+        ],
         compiler_params=params(16),
         cost_estimate=cost(150_000_000, 2_500_000),
         name="append",
@@ -282,7 +308,8 @@
     marks = []
     for u in range(NC * SEG_DEV):
         seg = jnp.broadcast_to(use[:, u : u + 1], (HALF, DH))
-        marks.append((seg, jnp.where(lane >= DH - ACT, use[:, 4:5], seg)))
+        edge = jnp.where(lane >= DH - ACT, use[:, 4:5], seg)
+        marks.append((seg.astype(BF), edge.astype(BF)))
 
     def stored(c, src, h):
         cs = slice(h * DH, (h + 1) * DH)
@@ -292,7 +319,7 @@
             s = i * DH // SEG
             last = s == 0 and (i + 1) * DH == SEG
             mark = marks[c * SEG_DEV + s][1 if last else 0]
-            parts.append((weigh(logits[:, i * DH : (i + 1) * DH]) * mark).astype(BF))
+            parts.append(weigh(logits[:, i * DH : (i + 1) * DH]).astype(BF) * mark)
         wt = jnp.concatenate(parts, axis=1)
         return jnp.dot(wt, src[STORED : 2 * STORED, cs], preferred_element_type=F32)
 

time: 78.1 us -> 77.6 us (level)
  transfers between devices with their start and end apart: 3 -> 3, of which waited for: 2 -> 2; matrix products, arithmetic and copies ran while one was open for 0% -> 0% of each run, Pallas kernels for 5% -> 4%
where the time goes in v5:
time: 77.6 us; the launch traced here: 77.1 us
  blocking collectives  36.5 us (47%)
  starting transfers between devices  25.3 us (33%)
  Pallas kernels  10.5 us (14%)
  waiting for transfers between devices  3.43 us (4%)
    all_to_all x3, blocking collectives, exchange(): lax.all_to_all(x, axis, split_axis=0, concat_axis=0, tiled=True, axis_ind...  34.5 us
    all_to_all x2, starting transfers between devices, exchange(): lax.all_to_all(x, axis, split_axis=0, concat_axis=0, tiled=True, axis_ind...  23.4 us
    pallas_call x1, Pallas kernels, attend(): pl.pallas_call(attend_kernel, out_shape=(jax.ShapeDtypeStruct((NX, ZROWS,...  3.87 us
    all_to_all x2, waiting for transfers between devices, exchange(): lax.all_to_all(x, axis, split_axis=0, concat_axis=0, tiled=True, axis_ind...  3.43 us
    pallas_call x1, Pallas kernels, project(): pl.pallas_call(project_kernel, out_shape=(jax.ShapeDtypeStruct((NZ, MB, W...  2.62 us
    all_gather x1, blocking collectives, per_device(): fresh = lax.all_gather(fresh, 'core', axis=0).reshape(XC, ZROWS, DH)  1.98 us
    ppermute x1, starting transfers between devices, per_device(): theirs = lax.ppermute(mine, 'core', [(0, 1), (1, 0)])  1.92 us
    pallas_call x1, Pallas kernels, append(): pl.pallas_call(append_kernel, out_shape=(stored,) * 2, in_specs=[sspec()]...  1.66 us
  transfers between devices with their start and end apart: 3, of which 2 were waited for; matrix products, arithmetic and copies ran while one was open for 0% of the time, Pallas kernels for 4%

profile of v5, /device:TPU:6, one launch (start us, length us, event | category | flops | bytes accessed | tf_op | source)
XLA Modules:
  0.0 77.1 jit_solution(15617001629609072839)
XLA Ops:
  0.6 0.0 copy-start
  0.6 0.0 copy-start.1
  0.7 2.6 %project.1 = (bf16[16,8,384]{2,1,0:T(8,128)(2,1)}, bf16[2,16,256]{2,1,0:T(8,128)(2,1)}, s32[2,3]{1,0:T(2,128)}, bf16[8,128]{1,0:T(8,128)(2,1)}) custom-call(s32[4,128]{1,0:T(4,128)} %refs_0_.1, s32[4]{0:T(128)} %refs_1_.1, s32[256]{0:T(256)} %refs_2_.1, s32[4]{0:T(128)} %refs_3_.1, s32[1,128]{1,0:T(1,128)} %bitcast.7, bf16[8,1024]{1,0:T(8,128)(2,1)} %cand.1, ...), custom_call_target="tpu_custom_call" | custom-call | tf_op jit(solution)/shard_map/gather/project/pallas_call | solution.py:148
  3.3 0.0 copy-start.5
  3.3 18.9 %all-to-all-start = ((bf16[16,8,384]{2,1,0:T(8,128)(2,1)}), bf16[16,8,384]{2,1,0:T(8,128)(2,1)S(1)}, u32[]{:S(2)}, u32[]{:S(2)}) async-start(bf16[16,8,384]{2,1,0:T(8,128)(2,1)} %get-tuple-element.22), calls=%async_computation | async-start | bytes 196608 | tf_op jit(solution)/shard_map/gather/all_to_all | solution.py:463
  22.2 0.0 copy-start.6
  22.2 0.0 copy-done
  22.2 0.0 copy-done.1
  22.2 0.0 copy-done.5
  22.2 0.6 copy-done.6
  22.8 0.0 copy-start.2
  22.8 0.0 copy-start.4
  22.8 0.0 copy-start.8
  22.8 0.7 stage.1.mine
  23.5 1.9 %collective-permute-start = (bf16[2048,256]{1,0:T(8,128)(2,1)S(1)}, bf16[2048,256]{1,0:T(8,128)(2,1)S(1)}, u32[]{:S(2)}, u32[]{:S(2)}) collective-permute-start(bf16[2048,256]{1,0:T(8,128)(2,1)S(1)} %stage.1.mine), channel_id=1, source_target_pairs={{0,4},{4,0},{1,5},{5,1},{2,6},{6,2},{3,7},{7,3},{8,12},{12,8},{9,1... | collective-permute-start | bytes 3145736 | tf_op jit(solution)/shard_map/share/ppermute | solution.py:500
  25.4 0.0 copy-done.2
  25.5 0.0 copy-done.4
  25.5 0.0 copy-done.8
  25.5 0.5 gate.1
  26.0 1.3 %all-to-all-done = bf16[16,8,384]{2,1,0:T(8,128)(2,1)S(1)} async-done(((bf16[16,8,384]{2,1,0:T(8,128)(2,1)}), bf16[16,8,384]{2,1,0:T(8,128)(2,1)S(1)}, u32[]{:S(2)}, u32[]{:S(2)}) %all-to-all-start) | async-done | bytes 98336 | tf_op jit(solution)/shard_map/gather/all_to_all | solution.py:463
  27.3 0.0 copy-start.7
  27.3 9.9 %all_to_all.31.arr = bf16[4,128,384]{2,1,0:T(8,128)(2,1)S(1)} all-to-all(bf16[4,128,384]{2,1,0:T(8,128)(2,1)S(1)} %spread.1), channel_id=1, replica_groups={{16,24,0,8},{17,25,1,9},{18,26,2,10},{19,27,3,11},{20,28,4,12},{21,29,5..., dimensions={0} | all-to-all | bytes 786432 | tf_op jit(solution)/shard_map/gather/all_to_all | solution.py:463
  37.2 0.0 collective-permute-done.other
  37.2 0.0 copy-done.7
  37.3 3.9 %attend.1 = (bf16[4,128,256]{2,1,0:T(8,128)(2,1)}, bf16[4,128,128]{2,1,0:T(8,128)(2,1)S(1)}) custom-call(bf16[8,128]{1,0:T(8,128)(2,1)S(1)} %copy-done.7, bf16[4,128,384]{2,1,0:T(8,128)(2,1)S(1)} %all_to_all.31.arr, bf16[2048,256]{1,0:T(8,128)(2,1)S(1)} %stage.1.mine, bf16[2048,256]{1,0:T(8,128)(2,1)S(1)} %collective-permute-done.other), custom_call_target="tpu_custom_call" | custom-call | tf_op jit(solution)/shard_map/attend/attend/pallas_call | solution.py:338
  41.1 4.5 %all-to-all-start.2 = ((bf16[4,128,256]{2,1,0:T(8,128)(2,1)}), bf16[4,128,256]{2,1,0:T(8,128)(2,1)S(1)}, u32[]{:S(2)}, u32[]{:S(2)}) async-start(bf16[4,128,256]{2,1,0:T(8,128)(2,1)} %get-tuple-element.29), calls=%async_computation.2 | async-start | bytes 524288 | tf_op jit(solution)/shard_map/return/all_to_all | solution.py:463
  45.6 2.0 %all-gather.arr = bf16[8,128,128]{2,1,0:T(8,128)(2,1)S(1)} all-gather(bf16[4,128,128]{2,1,0:T(8,128)(2,1)S(1)} %get-tuple-element.30), channel_id=2, replica_groups=mesh['z'=16,'x'=4,'core'=2,'mp'=4] {'core'}, dimensions={0}, use_global_device_ids=true | all-gather | bytes 393216 | tf_op jit(solution)/shard_map/append/all_gather | solution.py:512
  47.6 0.0 copy-start.3
  47.6 1.7 %append.1 = (bf16[1024,256]{1,0:T(8,128)(2,1)}, bf16[1024,256]{1,0:T(8,128)(2,1)}) custom-call(s32[2,3]{1,0:T(2,128)S(1)} %copy-done.6, bf16[8,128,128]{2,1,0:T(8,128)(2,1)S(1)} %all-gather.arr, bf16[1024,256]{1,0:T(8,128)(2,1)S(1)} %copy-done, bf16[1024,256]{1,0:T(8,128)(2,1)S(1)} %copy-done.1), custom_call_target="tpu_custom_call" | custom-call | flops 150000000 | bytes 2500000 | tf_op jit(solution)/shard_map/append/append/pallas_call | solution.py:270
  49.3 2.2 %all-to-all-done.2.arr = bf16[4,128,256]{2,1,0:T(8,128)(2,1)S(1)} async-done(((bf16[4,128,256]{2,1,0:T(8,128)(2,1)}), bf16[4,128,256]{2,1,0:T(8,128)(2,1)S(1)}, u32[]{:S(2)}, u32[]{:S(2)}) %all-to-all-start.2) | async-done | bytes 262176 | tf_op jit(solution)/shard_map/return/all_to_all | solution.py:463
  51.5 15.5 %all_to_all.32 = bf16[16,8,256]{2,1,0:T(8,128)(2,1)S(1)} all-to-all(bf16[16,8,256]{2,1,0:T(8,128)(2,1)S(1)} %bitcast.5), channel_id=1, replica_groups={{256,288,320,352,384,416,448,480,0,32,64,96,128,160,192,224},{257,289,3..., dimensions={0} | all-to-all | bytes 131072 | tf_op jit(solution)/shard_map/return/all_to_all | solution.py:463
  67.0 0.0 copy-done.3
  67.0 0.3 mix.1
  67.3 9.0 %all_to_all.33.arr = f32[4,8,640]{2,1,0:T(8,128)S(1)} all-to-all(f32[4,8,640]{2,1,0:T(8,128)S(1)} %mix.1), channel_id=1, replica_groups={{3,0,1,2},{7,4,5,6},{11,8,9,10},{15,12,13,14},{19,16,17,18},{23,20,21,2..., dimensions={0} | all-to-all | bytes 163840 | tf_op jit(solution)/shard_map/mix/all_to_all | solution.py:463
  76.4 0.8 finish.1
  (2 shorter events, 0.1 us)
Async XLA Ops:
  0.6 21.5 %copy-start = (bf16[1024,256]{1,0:T(8,128)(2,1)S(1)}, bf16[1024,256]{1,0:T(8,128)(2,1)}, u32[]{:S(2)}) copy-start(bf16[1024,256]{1,0:T(8,128)(2,1)} %keys.3) | copy-start | bytes 1572868
  0.6 21.5 %copy-start.1 = (bf16[1024,256]{1,0:T(8,128)(2,1)S(1)}, bf16[1024,256]{1,0:T(8,128)(2,1)}, u32[]{:S(2)}) copy-start(bf16[1024,256]{1,0:T(8,128)(2,1)} %vals.3) | copy-start | bytes 1572868
  3.3 18.9 %copy-start.5 = (bf16[2,16,256]{2,1,0:T(8,128)(2,1)S(1)}, bf16[2,16,256]{2,1,0:T(8,128)(2,1)}, u32[]{:S(2)}) copy-start(bf16[2,16,256]{2,1,0:T(8,128)(2,1)} %get-tuple-element.28.own) | copy-start | bytes 49156
  3.3 24.0 %all-to-all-start = ((bf16[16,8,384]{2,1,0:T(8,128)(2,1)}), bf16[16,8,384]{2,1,0:T(8,128)(2,1)S(1)}, u32[]{:S(2)}, u32[]{:S(2)}) async-start(bf16[16,8,384]{2,1,0:T(8,128)(2,1)} %get-tuple-element.22), calls=%async_computation | async-start | bytes 196608 | tf_op jit(solution)/shard_map/gather/all_to_all | solution.py:463
  22.2 0.7 copy-start.6
  22.8 2.6 %copy-start.2 = (bf16[256,1024]{1,0:T(8,128)(2,1)S(1)}, bf16[256,1024]{1,0:T(8,128)(2,1)}, u32[]{:S(2)}) copy-start(bf16[256,1024]{1,0:T(8,128)(2,1)} %wo.3) | copy-start | bytes 1572868
  22.8 2.6 %copy-start.4 = (bf16[8,1024]{1,0:T(8,128)(2,1)S(1)}, bf16[8,1024]{1,0:T(8,128)(2,1)}, u32[]{:S(2)}) copy-start(bf16[8,1024]{1,0:T(8,128)(2,1)} %cand.1) | copy-start | bytes 49156
  22.8 2.6 %copy-start.8 = (bf16[1024,256]{1,0:T(8,128)(2,1)S(1)}, bf16[1024,256]{1,0:T(8,128)(2,1)}, u32[]{:S(2)}) copy-start(bf16[1024,256]{1,0:T(8,128)(2,1)} %wg.1) | copy-start | bytes 1572868
  23.5 13.7 %collective-permute-start = (bf16[2048,256]{1,0:T(8,128)(2,1)S(1)}, bf16[2048,256]{1,0:T(8,128)(2,1)S(1)}, u32[]{:S(2)}, u32[]{:S(2)}) collective-permute-start(bf16[2048,256]{1,0:T(8,128)(2,1)S(1)} %stage.1.mine), channel_id=1, source_target_pairs={{0,4},{4,0},{1,5},{5,1},{2,6},{6,2},{3,7},{7,3},{8,12},{12,8},{9,1... | collective-permute-start | bytes 3145736 | tf_op jit(solution)/shard_map/share/ppermute | solution.py:500
  27.3 9.9 %copy-start.7 = (bf16[8,128]{1,0:T(8,128)(2,1)S(1)}, bf16[8,128]{1,0:T(8,128)(2,1)}, u32[]{:S(2)}) copy-start(bf16[8,128]{1,0:T(8,128)(2,1)} %get-tuple-element.21.maskrow) | copy-start | bytes 6148
  41.1 10.3 %all-to-all-start.2 = ((bf16[4,128,256]{2,1,0:T(8,128)(2,1)}), bf16[4,128,256]{2,1,0:T(8,128)(2,1)S(1)}, u32[]{:S(2)}, u32[]{:S(2)}) async-start(bf16[4,128,256]{2,1,0:T(8,128)(2,1)} %get-tuple-element.29), calls=%async_computation.2 | async-start | bytes 524288 | tf_op jit(solution)/shard_map/return/all_to_all | solution.py:463
  47.6 19.4 %copy-start.3 = (bf16[256,1024]{1,0:T(8,128)(2,1)S(1)}, bf16[256,1024]{1,0:T(8,128)(2,1)}, u32[]{:S(2)}) copy-start(bf16[256,1024]{1,0:T(8,128)(2,1)} %wo.3) | copy-start | bytes 1572868

commit v6 on v5

--- a/solution.py
+++ b/solution.py
@@ -70,16 +70,20 @@
 
 def project_kernel(*refs):
     small, big, outs = refs[:5], refs[5:10], refs[10:14]
-    scalars, vectors, weights = refs[14:18], refs[18:20], refs[20:25]
-    rows, block, marks, sems = refs[25:]
+    scalars, vectors, weights = refs[14:18], refs[18:20], refs[20:23]
+    rows, block, marks, sems = refs[23:]
     msg, own, info, mask = outs
-    heavy = [pltpu.make_async_copy(x, y, sems.at[i]) for i, (x, y) in enumerate(zip(big, weights))]
+    cand, act = big[:2]
+    heavy = [
+        pltpu.make_async_copy(x, y, sems.at[i])
+        for i, (x, y) in enumerate(zip(big[2:], weights))
+    ]
     sources = small[:4] + (small[0], small[4])
     light = [
-        pltpu.make_async_copy(x, y, sems.at[5 + i])
+        pltpu.make_async_copy(x, y, sems.at[3 + i])
         for i, (x, y) in enumerate(zip(sources, scalars + vectors))
     ]
-    for copy in heavy[:2] + light + heavy[2:]:
+    for copy in heavy[:1] + light + heavy[1:]:
         copy.start()
     block[...] = jnp.zeros_like(block)
     marks[...] = jnp.zeros_like(marks)
@@ -117,15 +121,13 @@
     marks[4:5] = jnp.where(users == act_user, 1.0, 0.0)
     mask[...] = marks[...].astype(BF)
 
-    c, q, a, k, v = weights
+    q, k, v = weights
     heavy[0].wait()
+    query = jnp.dot(cand[...], q[...], preferred_element_type=F32).astype(BF)
     heavy[1].wait()
-    query = jnp.dot(c[...], q[...], preferred_element_type=F32).astype(BF)
+    key = jnp.dot(act[...], k[...], preferred_element_type=F32)
     heavy[2].wait()
-    heavy[3].wait()
-    key = jnp.dot(a[...], k[...], preferred_element_type=F32)
-    heavy[4].wait()
-    value = jnp.dot(a[...], v[...], preferred_element_type=F32)
+    value = jnp.dot(act[...], v[...], preferred_element_type=F32)
     block[0:2] = key
     block[2:4] = value
     for h in range(HEADS):
@@ -153,7 +155,7 @@
             jax.ShapeDtypeStruct((SEG_DEV, 3), jnp.int32),
             jax.ShapeDtypeStruct((8, BATCHES), BF),
         ),
-        in_specs=[aspec()] * 10,
+        in_specs=[aspec()] * 5 + [vspec()] * 2 + [aspec()] * 3,
         out_specs=(vspec(), vspec(), sspec(), vspec()),
         scratch_shapes=[
             pltpu.SMEM(lists.shape, jnp.int32),
@@ -162,18 +164,16 @@
             pltpu.SMEM(news.shape, jnp.int32),
             pltpu.VMEM(lists.shape, jnp.int32),
             pltpu.VMEM((1, BATCHES), jnp.int32),
-            pltpu.VMEM((MB, D), BF),
             weight,
-            pltpu.VMEM((ACT, D), BF),
             weight,
             weight,
             pltpu.VMEM((MB, DH), F32),
             pltpu.VMEM((OWN, W), F32),
             pltpu.VMEM((8, BATCHES), F32),
-            pltpu.SemaphoreType.DMA((11,)),
+            pltpu.SemaphoreType.DMA((9,)),
         ],
         name="project",
-    )(lists, counts, lengths, news, users.reshape(1, BATCHES), cand, wq, act, wk, wv)
+    )(lists, counts, lengths, news, users.reshape(1, BATCHES), cand, act, wq, wk, wv)
 
 
 def stage_kernel(info, own, keys, vals, out):

time: 77.6 us -> 78.3 us (level)
  no operation moved by 1% of the time
where the time goes in v6:
time: 78.3 us; the launch traced here: 77.8 us
  blocking collectives  36.5 us (47%)
  starting transfers between devices  25.3 us (32%)
  Pallas kernels  11.2 us (14%)
  waiting for transfers between devices  3.43 us (4%)
    all_to_all x3, blocking collectives, exchange(): lax.all_to_all(x, axis, split_axis=0, concat_axis=0, tiled=True, axis_ind...  34.5 us
    all_to_all x2, starting transfers between devices, exchange(): lax.all_to_all(x, axis, split_axis=0, concat_axis=0, tiled=True, axis_ind...  23.4 us
    pallas_call x1, Pallas kernels, attend(): pl.pallas_call(attend_kernel, out_shape=(jax.ShapeDtypeStruct((NX, ZROWS,...  3.87 us
    all_to_all x2, waiting for transfers between devices, exchange(): lax.all_to_all(x, axis, split_axis=0, concat_axis=0, tiled=True, axis_ind...  3.43 us
    pallas_call x1, Pallas kernels, project(): pl.pallas_call(project_kernel, out_shape=(jax.ShapeDtypeStruct((NZ, MB, W...  3.29 us
    all_gather x1, blocking collectives, per_device(): fresh = lax.all_gather(fresh, 'core', axis=0).reshape(XC, ZROWS, DH)  1.98 us
    ppermute x1, starting transfers between devices, per_device(): theirs = lax.ppermute(mine, 'core', [(0, 1), (1, 0)])  1.92 us
    pallas_call x1, Pallas kernels, append(): pl.pallas_call(append_kernel, out_shape=(stored,) * 2, in_specs=[sspec()]...  1.66 us
  transfers between devices with their start and end apart: 3, of which 2 were waited for; matrix products, arithmetic and copies ran while one was open for 0% of the time, Pallas kernels for 4%

profile of v6, /device:TPU:6, one launch (start us, length us, event | category | flops | bytes accessed | tf_op | source)
XLA Modules:
  0.0 77.8 jit_solution(548077743096535755)
XLA Ops:
  0.6 0.0 copy-start
  0.6 0.0 copy-start.1
  0.7 3.3 %project.1 = (bf16[16,8,384]{2,1,0:T(8,128)(2,1)}, bf16[2,16,256]{2,1,0:T(8,128)(2,1)}, s32[2,3]{1,0:T(2,128)}, bf16[8,128]{1,0:T(8,128)(2,1)}) custom-call(s32[4,128]{1,0:T(4,128)} %refs_0_.1, s32[4]{0:T(128)} %refs_1_.1, s32[256]{0:T(256)} %refs_2_.1, s32[4]{0:T(128)} %refs_3_.1, s32[1,128]{1,0:T(1,128)} %bitcast.7, bf16[8,1024]{1,0:T(8,128)(2,1)} %cand.1, ...), custom_call_target="tpu_custom_call" | custom-call | tf_op jit(solution)/shard_map/gather/project/pallas_call | solution.py:150
  4.0 0.0 copy-start.5
  4.0 18.9 %all-to-all-start = ((bf16[16,8,384]{2,1,0:T(8,128)(2,1)}), bf16[16,8,384]{2,1,0:T(8,128)(2,1)S(1)}, u32[]{:S(2)}, u32[]{:S(2)}) async-start(bf16[16,8,384]{2,1,0:T(8,128)(2,1)} %get-tuple-element.22), calls=%async_computation | async-start | bytes 196608 | tf_op jit(solution)/shard_map/gather/all_to_all | solution.py:463
  22.8 0.0 copy-start.6
  22.8 0.0 copy-done
  22.8 0.0 copy-done.1
  22.9 0.0 copy-done.5
  22.9 0.6 copy-done.6
  23.5 0.0 copy-start.2
  23.5 0.0 copy-start.4
  23.5 0.0 copy-start.8
  23.5 0.7 stage.1.mine
  24.2 1.9 %collective-permute-start = (bf16[2048,256]{1,0:T(8,128)(2,1)S(1)}, bf16[2048,256]{1,0:T(8,128)(2,1)S(1)}, u32[]{:S(2)}, u32[]{:S(2)}) collective-permute-start(bf16[2048,256]{1,0:T(8,128)(2,1)S(1)} %stage.1.mine), channel_id=1, source_target_pairs={{0,4},{4,0},{1,5},{5,1},{2,6},{6,2},{3,7},{7,3},{8,12},{12,8},{9,1... | collective-permute-start | bytes 3145736 | tf_op jit(solution)/shard_map/share/ppermute | solution.py:500
  26.1 0.0 copy-done.2
  26.1 0.0 copy-done.4
  26.1 0.0 copy-done.8
  26.1 0.5 gate.1
  26.7 1.3 %all-to-all-done = bf16[16,8,384]{2,1,0:T(8,128)(2,1)S(1)} async-done(((bf16[16,8,384]{2,1,0:T(8,128)(2,1)}), bf16[16,8,384]{2,1,0:T(8,128)(2,1)S(1)}, u32[]{:S(2)}, u32[]{:S(2)}) %all-to-all-start) | async-done | bytes 98336 | tf_op jit(solution)/shard_map/gather/all_to_all | solution.py:463
  28.0 0.0 copy-start.7
  28.0 9.9 %all_to_all.31.arr = bf16[4,128,384]{2,1,0:T(8,128)(2,1)S(1)} all-to-all(bf16[4,128,384]{2,1,0:T(8,128)(2,1)S(1)} %spread.1), channel_id=1, replica_groups={{16,24,0,8},{17,25,1,9},{18,26,2,10},{19,27,3,11},{20,28,4,12},{21,29,5..., dimensions={0} | all-to-all | bytes 786432 | tf_op jit(solution)/shard_map/gather/all_to_all | solution.py:463
  37.9 0.0 collective-permute-done.other
  37.9 0.0 copy-done.7
  37.9 3.9 %attend.1 = (bf16[4,128,256]{2,1,0:T(8,128)(2,1)}, bf16[4,128,128]{2,1,0:T(8,128)(2,1)S(1)}) custom-call(bf16[8,128]{1,0:T(8,128)(2,1)S(1)} %copy-done.7, bf16[4,128,384]{2,1,0:T(8,128)(2,1)S(1)} %all_to_all.31.arr, bf16[2048,256]{1,0:T(8,128)(2,1)S(1)} %stage.1.mine, bf16[2048,256]{1,0:T(8,128)(2,1)S(1)} %collective-permute-done.other), custom_call_target="tpu_custom_call" | custom-call | tf_op jit(solution)/shard_map/attend/attend/pallas_call | solution.py:338
  41.8 4.5 %all-to-all-start.2 = ((bf16[4,128,256]{2,1,0:T(8,128)(2,1)}), bf16[4,128,256]{2,1,0:T(8,128)(2,1)S(1)}, u32[]{:S(2)}, u32[]{:S(2)}) async-start(bf16[4,128,256]{2,1,0:T(8,128)(2,1)} %get-tuple-element.29), calls=%async_computation.2 | async-start | bytes 524288 | tf_op jit(solution)/shard_map/return/all_to_all | solution.py:463
  46.3 2.0 %all-gather.arr = bf16[8,128,128]{2,1,0:T(8,128)(2,1)S(1)} all-gather(bf16[4,128,128]{2,1,0:T(8,128)(2,1)S(1)} %get-tuple-element.30), channel_id=2, replica_groups=mesh['z'=16,'x'=4,'core'=2,'mp'=4] {'core'}, dimensions={0}, use_global_device_ids=true | all-gather | bytes 393216 | tf_op jit(solution)/shard_map/append/all_gather | solution.py:512
  48.3 0.0 copy-start.3
  48.3 1.7 %append.1 = (bf16[1024,256]{1,0:T(8,128)(2,1)}, bf16[1024,256]{1,0:T(8,128)(2,1)}) custom-call(s32[2,3]{1,0:T(2,128)S(1)} %copy-done.6, bf16[8,128,128]{2,1,0:T(8,128)(2,1)S(1)} %all-gather.arr, bf16[1024,256]{1,0:T(8,128)(2,1)S(1)} %copy-done, bf16[1024,256]{1,0:T(8,128)(2,1)S(1)} %copy-done.1), custom_call_target="tpu_custom_call" | custom-call | flops 150000000 | bytes 2500000 | tf_op jit(solution)/shard_map/append/append/pallas_call | solution.py:270
  49.9 2.2 %all-to-all-done.2.arr = bf16[4,128,256]{2,1,0:T(8,128)(2,1)S(1)} async-done(((bf16[4,128,256]{2,1,0:T(8,128)(2,1)}), bf16[4,128,256]{2,1,0:T(8,128)(2,1)S(1)}, u32[]{:S(2)}, u32[]{:S(2)}) %all-to-all-start.2) | async-done | bytes 262176 | tf_op jit(solution)/shard_map/return/all_to_all | solution.py:463
  52.2 15.5 %all_to_all.32 = bf16[16,8,256]{2,1,0:T(8,128)(2,1)S(1)} all-to-all(bf16[16,8,256]{2,1,0:T(8,128)(2,1)S(1)} %bitcast.5), channel_id=1, replica_groups={{256,288,320,352,384,416,448,480,0,32,64,96,128,160,192,224},{257,289,3..., dimensions={0} | all-to-all | bytes 131072 | tf_op jit(solution)/shard_map/return/all_to_all | solution.py:463
  67.7 0.0 copy-done.3
  67.7 0.3 mix.1
  68.0 9.0 %all_to_all.33.arr = f32[4,8,640]{2,1,0:T(8,128)S(1)} all-to-all(f32[4,8,640]{2,1,0:T(8,128)S(1)} %mix.1), channel_id=1, replica_groups={{3,0,1,2},{7,4,5,6},{11,8,9,10},{15,12,13,14},{19,16,17,18},{23,20,21,2..., dimensions={0} | all-to-all | bytes 163840 | tf_op jit(solution)/shard_map/mix/all_to_all | solution.py:463
  77.0 0.8 finish.1
  (2 shorter events, 0.1 us)
Async XLA Ops:
  0.6 22.2 %copy-start = (bf16[1024,256]{1,0:T(8,128)(2,1)S(1)}, bf16[1024,256]{1,0:T(8,128)(2,1)}, u32[]{:S(2)}) copy-start(bf16[1024,256]{1,0:T(8,128)(2,1)} %keys.3) | copy-start | bytes 1572868
  0.6 22.2 %copy-start.1 = (bf16[1024,256]{1,0:T(8,128)(2,1)S(1)}, bf16[1024,256]{1,0:T(8,128)(2,1)}, u32[]{:S(2)}) copy-start(bf16[1024,256]{1,0:T(8,128)(2,1)} %vals.3) | copy-start | bytes 1572868
  4.0 18.9 %copy-start.5 = (bf16[2,16,256]{2,1,0:T(8,128)(2,1)S(1)}, bf16[2,16,256]{2,1,0:T(8,128)(2,1)}, u32[]{:S(2)}) copy-start(bf16[2,16,256]{2,1,0:T(8,128)(2,1)} %get-tuple-element.28.own) | copy-start | bytes 49156
  4.0 24.0 %all-to-all-start = ((bf16[16,8,384]{2,1,0:T(8,128)(2,1)}), bf16[16,8,384]{2,1,0:T(8,128)(2,1)S(1)}, u32[]{:S(2)}, u32[]{:S(2)}) async-start(bf16[16,8,384]{2,1,0:T(8,128)(2,1)} %get-tuple-element.22), calls=%async_computation | async-start | bytes 196608 | tf_op jit(solution)/shard_map/gather/all_to_all | solution.py:463
  22.8 0.7 copy-start.6
  23.5 2.6 %copy-start.2 = (bf16[256,1024]{1,0:T(8,128)(2,1)S(1)}, bf16[256,1024]{1,0:T(8,128)(2,1)}, u32[]{:S(2)}) copy-start(bf16[256,1024]{1,0:T(8,128)(2,1)} %wo.3) | copy-start | bytes 1572868
  23.5 2.6 %copy-start.4 = (bf16[8,1024]{1,0:T(8,128)(2,1)S(1)}, bf16[8,1024]{1,0:T(8,128)(2,1)}, u32[]{:S(2)}) copy-start(bf16[8,1024]{1,0:T(8,128)(2,1)} %cand.1) | copy-start | bytes 49156
  23.5 2.6 %copy-start.8 = (bf16[1024,256]{1,0:T(8,128)(2,1)S(1)}, bf16[1024,256]{1,0:T(8,128)(2,1)}, u32[]{:S(2)}) copy-start(bf16[1024,256]{1,0:T(8,128)(2,1)} %wg.1) | copy-start | bytes 1572868
  24.2 13.7 %collective-permute-start = (bf16[2048,256]{1,0:T(8,128)(2,1)S(1)}, bf16[2048,256]{1,0:T(8,128)(2,1)S(1)}, u32[]{:S(2)}, u32[]{:S(2)}) collective-permute-start(bf16[2048,256]{1,0:T(8,128)(2,1)S(1)} %stage.1.mine), channel_id=1, source_target_pairs={{0,4},{4,0},{1,5},{5,1},{2,6},{6,2},{3,7},{7,3},{8,12},{12,8},{9,1... | collective-permute-start | bytes 3145736 | tf_op jit(solution)/shard_map/share/ppermute | solution.py:500
  28.0 9.9 %copy-start.7 = (bf16[8,128]{1,0:T(8,128)(2,1)S(1)}, bf16[8,128]{1,0:T(8,128)(2,1)}, u32[]{:S(2)}) copy-start(bf16[8,128]{1,0:T(8,128)(2,1)} %get-tuple-element.21.maskrow) | copy-start | bytes 6148
  41.8 10.3 %all-to-all-start.2 = ((bf16[4,128,256]{2,1,0:T(8,128)(2,1)}), bf16[4,128,256]{2,1,0:T(8,128)(2,1)S(1)}, u32[]{:S(2)}, u32[]{:S(2)}) async-start(bf16[4,128,256]{2,1,0:T(8,128)(2,1)} %get-tuple-element.29), calls=%async_computation.2 | async-start | bytes 524288 | tf_op jit(solution)/shard_map/return/all_to_all | solution.py:463
  48.3 19.4 %copy-start.3 = (bf16[256,1024]{1,0:T(8,128)(2,1)S(1)}, bf16[256,1024]{1,0:T(8,128)(2,1)}, u32[]{:S(2)}) copy-start(bf16[256,1024]{1,0:T(8,128)(2,1)} %wo.3) | copy-start | bytes 1572868

commit v7 on v6

--- a/solution.py
+++ b/solution.py
@@ -29,7 +29,7 @@
 HALF = ZX * MB
 ZROWS = NZ * MB
 FIRST_Z = 8
-FIRST_X = 2
+FIRST_X = 3
 FIRST_Y = 3
 STORED = SEG_DEV * SEG
 OWN = 16

time: 78.3 us -> 78.5 us (level)
  starting transfers between devices: 25.3 us -> 24.2 us
  waiting for transfers between devices: 3.43 us -> 4.23 us
    all_to_all x2, starting transfers between devices: 23.4 us -> 22.3 us  [exchange(): lax.all_to_all(x, axis, split_axis=0, concat_axis=0, tiled=True, axis_ind...]
    all_to_all x2, waiting for transfers between devices: 3.43 us -> 4.23 us  [exchange(): lax.all_to_all(x, axis, split_axis=0, concat_axis=0, tiled=True, axis_ind...]
where the time goes in v7:
time: 78.5 us; the launch traced here: 77.8 us
  blocking collectives  36.8 us (47%)
  starting transfers between devices  24.2 us (31%)
  Pallas kernels  11.2 us (14%)
  waiting for transfers between devices  4.23 us (5%)
    all_to_all x3, blocking collectives, exchange(): lax.all_to_all(x, axis, split_axis=0, concat_axis=0, tiled=True, axis_ind...  34.8 us
    all_to_all x2, starting transfers between devices, exchange(): lax.all_to_all(x, axis, split_axis=0, concat_axis=0, tiled=True, axis_ind...  22.3 us
    all_to_all x2, waiting for transfers between devices, exchange(): lax.all_to_all(x, axis, split_axis=0, concat_axis=0, tiled=True, axis_ind...  4.23 us
    pallas_call x1, Pallas kernels, attend(): pl.pallas_call(attend_kernel, out_shape=(jax.ShapeDtypeStruct((NX, ZROWS,...  3.87 us
    pallas_call x1, Pallas kernels, project(): pl.pallas_call(project_kernel, out_shape=(jax.ShapeDtypeStruct((NZ, MB, W...  3.29 us
    all_gather x1, blocking collectives, per_device(): fresh = lax.all_gather(fresh, 'core', axis=0).reshape(XC, ZROWS, DH)  1.99 us
    ppermute x1, starting transfers between devices, per_device(): theirs = lax.ppermute(mine, 'core', [(0, 1), (1, 0)])  1.92 us
    pallas_call x1, Pallas kernels, append(): pl.pallas_call(append_kernel, out_shape=(stored,) * 2, in_specs=[sspec()]...  1.66 us
  transfers between devices with their start and end apart: 3, of which 2 were waited for; matrix products, arithmetic and copies ran while one was open for 0% of the time, Pallas kernels for 4%

profile of v7, /device:TPU:6, one launch (start us, length us, event | category | flops | bytes accessed | tf_op | source)
XLA Modules:
  0.0 77.8 jit_solution(11601547382247015783)
XLA Ops:
  0.6 0.0 copy-start
  0.6 0.0 copy-start.1
  0.7 3.3 %project.1 = (bf16[16,8,384]{2,1,0:T(8,128)(2,1)}, bf16[2,16,256]{2,1,0:T(8,128)(2,1)}, s32[2,3]{1,0:T(2,128)}, bf16[8,128]{1,0:T(8,128)(2,1)}) custom-call(s32[4,128]{1,0:T(4,128)} %refs_0_.1, s32[4]{0:T(128)} %refs_1_.1, s32[256]{0:T(256)} %refs_2_.1, s32[4]{0:T(128)} %refs_3_.1, s32[1,128]{1,0:T(1,128)} %bitcast.7, bf16[8,1024]{1,0:T(8,128)(2,1)} %cand.1, ...), custom_call_target="tpu_custom_call" | custom-call | tf_op jit(solution)/shard_map/gather/project/pallas_call | solution.py:150
  4.0 0.0 copy-start.5
  4.0 18.9 %all-to-all-start = ((bf16[16,8,384]{2,1,0:T(8,128)(2,1)}), bf16[16,8,384]{2,1,0:T(8,128)(2,1)S(1)}, u32[]{:S(2)}, u32[]{:S(2)}) async-start(bf16[16,8,384]{2,1,0:T(8,128)(2,1)} %get-tuple-element.22), calls=%async_computation | async-start | bytes 196608 | tf_op jit(solution)/shard_map/gather/all_to_all | solution.py:463
  22.8 0.0 copy-start.6
  22.8 0.0 copy-done
  22.8 0.0 copy-done.1
  22.9 0.0 copy-done.5
  22.9 0.6 copy-done.6
  23.5 0.0 copy-start.2
  23.5 0.0 copy-start.4
  23.5 0.0 copy-start.8
  23.5 0.7 stage.1.mine
  24.2 1.9 %collective-permute-start = (bf16[2048,256]{1,0:T(8,128)(2,1)S(1)}, bf16[2048,256]{1,0:T(8,128)(2,1)S(1)}, u32[]{:S(2)}, u32[]{:S(2)}) collective-permute-start(bf16[2048,256]{1,0:T(8,128)(2,1)S(1)} %stage.1.mine), channel_id=1, source_target_pairs={{0,4},{4,0},{1,5},{5,1},{2,6},{6,2},{3,7},{7,3},{8,12},{12,8},{9,1... | collective-permute-start | bytes 3145736 | tf_op jit(solution)/shard_map/share/ppermute | solution.py:500
  26.1 0.0 copy-done.2
  26.1 0.0 copy-done.4
  26.1 0.0 copy-done.8
  26.1 0.5 gate.1
  26.7 1.3 %all-to-all-done = bf16[16,8,384]{2,1,0:T(8,128)(2,1)S(1)} async-done(((bf16[16,8,384]{2,1,0:T(8,128)(2,1)}), bf16[16,8,384]{2,1,0:T(8,128)(2,1)S(1)}, u32[]{:S(2)}, u32[]{:S(2)}) %all-to-all-start) | async-done | bytes 98336 | tf_op jit(solution)/shard_map/gather/all_to_all | solution.py:463
  28.0 0.0 copy-start.7
  28.0 10.2 %all_to_all.31.arr = bf16[4,128,384]{2,1,0:T(8,128)(2,1)S(1)} all-to-all(bf16[4,128,384]{2,1,0:T(8,128)(2,1)S(1)} %spread.1), channel_id=1, replica_groups={{24,0,8,16},{25,1,9,17},{26,2,10,18},{27,3,11,19},{28,4,12,20},{29,5,13..., dimensions={0} | all-to-all | bytes 786432 | tf_op jit(solution)/shard_map/gather/all_to_all | solution.py:463
  38.2 0.0 collective-permute-done.other
  38.2 0.0 copy-done.7
  38.2 3.9 %attend.1 = (bf16[4,128,256]{2,1,0:T(8,128)(2,1)}, bf16[4,128,128]{2,1,0:T(8,128)(2,1)S(1)}) custom-call(bf16[8,128]{1,0:T(8,128)(2,1)S(1)} %copy-done.7, bf16[4,128,384]{2,1,0:T(8,128)(2,1)S(1)} %all_to_all.31.arr, bf16[2048,256]{1,0:T(8,128)(2,1)S(1)} %stage.1.mine, bf16[2048,256]{1,0:T(8,128)(2,1)S(1)} %collective-permute-done.other), custom_call_target="tpu_custom_call" | custom-call | tf_op jit(solution)/shard_map/attend/attend/pallas_call | solution.py:338
  42.1 3.4 %all-to-all-start.2 = ((bf16[4,128,256]{2,1,0:T(8,128)(2,1)}), bf16[4,128,256]{2,1,0:T(8,128)(2,1)S(1)}, u32[]{:S(2)}, u32[]{:S(2)}) async-start(bf16[4,128,256]{2,1,0:T(8,128)(2,1)} %get-tuple-element.29), calls=%async_computation.2 | async-start | bytes 524288 | tf_op jit(solution)/shard_map/return/all_to_all | solution.py:463
  45.5 2.0 %all-gather.arr = bf16[8,128,128]{2,1,0:T(8,128)(2,1)S(1)} all-gather(bf16[4,128,128]{2,1,0:T(8,128)(2,1)S(1)} %get-tuple-element.30), channel_id=2, replica_groups=mesh['z'=16,'x'=4,'core'=2,'mp'=4] {'core'}, dimensions={0}, use_global_device_ids=true | all-gather | bytes 393216 | tf_op jit(solution)/shard_map/append/all_gather | solution.py:512
  47.5 0.0 copy-start.3
  47.5 1.7 %append.1 = (bf16[1024,256]{1,0:T(8,128)(2,1)}, bf16[1024,256]{1,0:T(8,128)(2,1)}) custom-call(s32[2,3]{1,0:T(2,128)S(1)} %copy-done.6, bf16[8,128,128]{2,1,0:T(8,128)(2,1)S(1)} %all-gather.arr, bf16[1024,256]{1,0:T(8,128)(2,1)S(1)} %copy-done, bf16[1024,256]{1,0:T(8,128)(2,1)S(1)} %copy-done.1), custom_call_target="tpu_custom_call" | custom-call | flops 150000000 | bytes 2500000 | tf_op jit(solution)/shard_map/append/append/pallas_call | solution.py:270
  49.2 3.0 %all-to-all-done.2.arr = bf16[4,128,256]{2,1,0:T(8,128)(2,1)S(1)} async-done(((bf16[4,128,256]{2,1,0:T(8,128)(2,1)}), bf16[4,128,256]{2,1,0:T(8,128)(2,1)S(1)}, u32[]{:S(2)}, u32[]{:S(2)}) %all-to-all-start.2) | async-done | bytes 262176 | tf_op jit(solution)/shard_map/return/all_to_all | solution.py:463
  52.2 15.5 %all_to_all.32 = bf16[16,8,256]{2,1,0:T(8,128)(2,1)S(1)} all-to-all(bf16[16,8,256]{2,1,0:T(8,128)(2,1)S(1)} %bitcast.5), channel_id=1, replica_groups={{256,288,320,352,384,416,448,480,0,32,64,96,128,160,192,224},{257,289,3..., dimensions={0} | all-to-all | bytes 131072 | tf_op jit(solution)/shard_map/return/all_to_all | solution.py:463
  67.7 0.0 copy-done.3
  67.7 0.3 mix.1
  68.0 9.0 %all_to_all.33.arr = f32[4,8,640]{2,1,0:T(8,128)S(1)} all-to-all(f32[4,8,640]{2,1,0:T(8,128)S(1)} %mix.1), channel_id=1, replica_groups={{3,0,1,2},{7,4,5,6},{11,8,9,10},{15,12,13,14},{19,16,17,18},{23,20,21,2..., dimensions={0} | all-to-all | bytes 163840 | tf_op jit(solution)/shard_map/mix/all_to_all | solution.py:463
  77.1 0.8 finish.1
  (2 shorter events, 0.1 us)
Async XLA Ops:
  0.6 22.2 %copy-start = (bf16[1024,256]{1,0:T(8,128)(2,1)S(1)}, bf16[1024,256]{1,0:T(8,128)(2,1)}, u32[]{:S(2)}) copy-start(bf16[1024,256]{1,0:T(8,128)(2,1)} %keys.3) | copy-start | bytes 1572868
  0.6 22.2 %copy-start.1 = (bf16[1024,256]{1,0:T(8,128)(2,1)S(1)}, bf16[1024,256]{1,0:T(8,128)(2,1)}, u32[]{:S(2)}) copy-start(bf16[1024,256]{1,0:T(8,128)(2,1)} %vals.3) | copy-start | bytes 1572868
  4.0 18.9 %copy-start.5 = (bf16[2,16,256]{2,1,0:T(8,128)(2,1)S(1)}, bf16[2,16,256]{2,1,0:T(8,128)(2,1)}, u32[]{:S(2)}) copy-start(bf16[2,16,256]{2,1,0:T(8,128)(2,1)} %get-tuple-element.28.own) | copy-start | bytes 49156
  4.0 24.0 %all-to-all-start = ((bf16[16,8,384]{2,1,0:T(8,128)(2,1)}), bf16[16,8,384]{2,1,0:T(8,128)(2,1)S(1)}, u32[]{:S(2)}, u32[]{:S(2)}) async-start(bf16[16,8,384]{2,1,0:T(8,128)(2,1)} %get-tuple-element.22), calls=%async_computation | async-start | bytes 196608 | tf_op jit(solution)/shard_map/gather/all_to_all | solution.py:463
  22.8 0.7 copy-start.6
  23.5 2.6 %copy-start.2 = (bf16[256,1024]{1,0:T(8,128)(2,1)S(1)}, bf16[256,1024]{1,0:T(8,128)(2,1)}, u32[]{:S(2)}) copy-start(bf16[256,1024]{1,0:T(8,128)(2,1)} %wo.3) | copy-start | bytes 1572868
  23.5 2.6 %copy-start.4 = (bf16[8,1024]{1,0:T(8,128)(2,1)S(1)}, bf16[8,1024]{1,0:T(8,128)(2,1)}, u32[]{:S(2)}) copy-start(bf16[8,1024]{1,0:T(8,128)(2,1)} %cand.1) | copy-start | bytes 49156
  23.5 2.6 %copy-start.8 = (bf16[1024,256]{1,0:T(8,128)(2,1)S(1)}, bf16[1024,256]{1,0:T(8,128)(2,1)}, u32[]{:S(2)}) copy-start(bf16[1024,256]{1,0:T(8,128)(2,1)} %wg.1) | copy-start | bytes 1572868
  24.2 14.0 %collective-permute-start = (bf16[2048,256]{1,0:T(8,128)(2,1)S(1)}, bf16[2048,256]{1,0:T(8,128)(2,1)S(1)}, u32[]{:S(2)}, u32[]{:S(2)}) collective-permute-start(bf16[2048,256]{1,0:T(8,128)(2,1)S(1)} %stage.1.mine), channel_id=1, source_target_pairs={{0,4},{4,0},{1,5},{5,1},{2,6},{6,2},{3,7},{7,3},{8,12},{12,8},{9,1... | collective-permute-start | bytes 3145736 | tf_op jit(solution)/shard_map/share/ppermute | solution.py:500
  28.0 10.2 %copy-start.7 = (bf16[8,128]{1,0:T(8,128)(2,1)S(1)}, bf16[8,128]{1,0:T(8,128)(2,1)}, u32[]{:S(2)}) copy-start(bf16[8,128]{1,0:T(8,128)(2,1)} %get-tuple-element.21.maskrow) | copy-start | bytes 6148
  42.1 10.1 %all-to-all-start.2 = ((bf16[4,128,256]{2,1,0:T(8,128)(2,1)}), bf16[4,128,256]{2,1,0:T(8,128)(2,1)S(1)}, u32[]{:S(2)}, u32[]{:S(2)}) async-start(bf16[4,128,256]{2,1,0:T(8,128)(2,1)} %get-tuple-element.29), calls=%async_computation.2 | async-start | bytes 524288 | tf_op jit(solution)/shard_map/return/all_to_all | solution.py:463
  47.5 20.2 %copy-start.3 = (bf16[256,1024]{1,0:T(8,128)(2,1)S(1)}, bf16[256,1024]{1,0:T(8,128)(2,1)}, u32[]{:S(2)}) copy-start(bf16[256,1024]{1,0:T(8,128)(2,1)} %wo.3) | copy-start | bytes 1572868
